TPU v7x, 512 devices: a whole 4x8x8 slice. The times are simulated.
512 devices in a mesh: seq: 64 (over y, z), ffn: 8 (over x, core).
Axes of the slice: x: 4, y: 8, z: 8, core: 2. Of those that a mesh axis runs over, the one named last changes fastest.
Arguments:
- queries: bfloat16 [8192, 4096], P('seq', 'ffn'), may hold values from -256 to 256
- key_vectors: bfloat16 [8192, 512], P('seq', 'ffn'), may hold values from -7 to 7
- head_value_vectors: bfloat16 [8192, 512], P('seq', 'ffn'), may hold values from -6 to 6
- head_sink_logits: float32 [64], P('ffn'), may hold values from -5 to 5
- out_weight: bfloat16 [4096, 2880], P('ffn', 'seq'), may hold values from -0.09375 to 0.09375
- residual: bfloat16 [8192, 2880], P('seq', 'ffn'), may hold values from -6 to 6
- norm_gain: float32 [2880], P('ffn'), may hold values from 0.1 to 1.9
- router_weight: bfloat16 [2880, 64], P('ffn'), may hold values from -5 to 5
- expert_ids: int32 [8192, 4], P('seq'), may hold values from 0 to 63, all different within a row; in each aligned block of 128 rows (0 to 127, 128 to 255, ...) at most 16 rows name the same one
- gate_weight: bfloat16 [64, 2880, 1440], P('seq', None, 'ffn'), may hold values from -0.109375 to 0.109375
- up_weight: bfloat16 [64, 2880, 1440], P('seq', None, 'ffn'), may hold values from -0.109375 to 0.109375
- down_weight: bfloat16 [64, 1440, 2880], P('seq', None, 'ffn'), may hold values from -0.15625 to 0.15625
- cotangent: bfloat16 [8192, 2880], P('seq', 'ffn'), may hold values from -6 to 6
Outputs:
- layer_output: bfloat16 [8192, 2880], P('seq', 'ffn')
- grad_down: bfloat16 [64, 1440, 2880], P('seq', None, 'ffn')
Inputs may be any that keep to these rules, and one draw needn't show every extreme that they name: `expert_ids`: each token names 4 distinct experts. Within the 128 tokens of one index of seq no expert is named by more than 16 tokens, a bound that some block reaches.
All inputs are finite; a program needn't handle non-finite values.
Results may differ from a plain program's by a relative error of at most 0.0073.
Values may be sent and summed in bfloat16 or wider, within the bound.
No kernel may reach another device: no remote copies, remote signals or barrier semaphores. Data moves between devices by JAX's collectives and lax.ppermute only.
A program may use at most 64 MiB of HBM per device.

v0:
```python
import jax
import jax.numpy as jnp
from jax import lax
from jax.sharding import PartitionSpec as P

D = 2880
QUERY_HEADS = 64
KEY_VALUE_HEADS = 8
HEAD_SIZE = 64
VISIBLE_TOKENS = 128
TOPK = 4


def from_behind(value, axis, steps):
    count = lax.axis_size(axis)
    leading, last = (max(0, -steps), min(count, count - steps))
    return lax.ppermute(value, axis, [(source, source + steps) for source in range(leading, last)])


def body(
    queries,
    key_vectors,
    head_value_vectors,
    head_sink_logits,
    out_weight,
    residual,
    norm_gain,
    router_weight,
    expert_ids,
    gate_weight,
    up_weight,
    down_weight,
    cotangent,
):
    tok_rows = queries.shape[0]
    key_heads = key_vectors.shape[1] // HEAD_SIZE
    query_grouping = QUERY_HEADS // KEY_VALUE_HEADS
    prev_keys, prev_values = from_behind((key_vectors, head_value_vectors), "seq", 1)
    all_keys = jnp.concatenate([prev_keys, key_vectors], axis=0).reshape(
        2 * tok_rows, key_heads, HEAD_SIZE
    )
    all_values = jnp.concatenate([prev_values, head_value_vectors], axis=0).reshape(
        2 * tok_rows, key_heads, HEAD_SIZE
    )
    query_heads = queries.reshape(tok_rows, key_heads, query_grouping, HEAD_SIZE)
    scores = jnp.einsum(
        "tkgd,skd->kgts", query_heads, all_keys, preferred_element_type=jnp.float32
    ) * HEAD_SIZE ** (-0.5)
    offset = lax.axis_index("seq") * tok_rows
    query_pos = offset + jnp.arange(tok_rows, dtype=jnp.int32)
    key_pos = offset - tok_rows + jnp.arange(2 * tok_rows, dtype=jnp.int32)
    valid = (
        (key_pos[None, :] >= 0)
        & (key_pos[None, :] <= query_pos[:, None])
        & (key_pos[None, :] > query_pos[:, None] - VISIBLE_TOKENS)
    )
    scores = jnp.where(valid, scores, -1e30)
    sink_entries = head_sink_logits.reshape(key_heads, query_grouping)[:, :, None]
    highest = jnp.maximum(jnp.max(scores, axis=-1), sink_entries)
    powers = jnp.exp(scores - highest[..., None])
    denom = jnp.sum(powers, axis=-1) + jnp.exp(sink_entries - highest)
    weights = (powers / denom[..., None]).astype(jnp.bfloat16)
    attended = jnp.einsum("kgts,skd->tkgd", weights, all_values, preferred_element_type=jnp.float32)
    attended = attended.astype(jnp.bfloat16).reshape(
        tok_rows, key_heads * query_grouping * HEAD_SIZE
    )
    partial_out = jnp.dot(
        attended,
        lax.all_gather(out_weight, "seq", axis=1, tiled=True),
        preferred_element_type=jnp.float32,
    )
    updated = residual.astype(jnp.float32) + lax.psum_scatter(
        partial_out, "ffn", scatter_dimension=1, tiled=True
    )
    square_sum = jnp.sum(updated * updated, axis=-1)
    router_f32 = router_weight.astype(jnp.float32)
    total_sq = lax.psum(square_sum, "ffn")
    scaling = lax.rsqrt(total_sq / D + 1e-05)[:, None]
    normed = updated * scaling * norm_gain
    normed_rows = normed.astype(jnp.bfloat16)
    router_logits = lax.psum(jnp.dot(normed, router_f32, precision=lax.Precision.HIGHEST), "ffn")
    experts = router_weight.shape[1]
    capacity = 2 * TOPK * tok_rows // experts
    onehot = (expert_ids[:, :, None] == jnp.arange(experts, dtype=jnp.int32)).astype(jnp.float32)
    chosen = jnp.sum(onehot * router_logits[:, None, :], axis=-1)
    top_val = jnp.max(chosen, axis=-1, keepdims=True)
    gate_pow = jnp.exp(chosen - top_val)
    gates = (gate_pow / jnp.sum(gate_pow, axis=-1, keepdims=True)).astype(jnp.bfloat16)
    counts = jnp.sum(onehot, axis=1)
    row_index = jnp.arange(tok_rows, dtype=jnp.int32)
    strictly_lower = (row_index[:, None] > row_index[None, :]).astype(jnp.float32)
    before = jnp.dot(strictly_lower, counts, precision=lax.Precision.HIGHEST)
    slot = jnp.sum(onehot * before[:, None, :], axis=-1)
    slot_hot = (
        slot[:, :, None] == jnp.arange(capacity, dtype=jnp.int32).astype(jnp.float32)
    ).astype(jnp.float32)
    placing = (
        jnp.einsum("tje,tjc->tec", onehot, slot_hot)
        .reshape(tok_rows, experts * capacity)
        .astype(jnp.bfloat16)
    )
    combining = (
        jnp.einsum("tj,tje,tjc->tec", gates.astype(jnp.float32), onehot, slot_hot)
        .reshape(tok_rows, experts * capacity)
        .astype(jnp.bfloat16)
    )
    row_contract = (((0,), (0,)), ((), ()))
    full_rows = lax.all_gather(normed_rows, "ffn", axis=1, tiled=True)
    local_slots = lax.dot_general(
        placing, full_rows, row_contract, preferred_element_type=jnp.float32
    )
    local_slots = local_slots.astype(jnp.bfloat16).reshape(experts, capacity, D)
    arrived = lax.all_to_all(local_slots, "seq", split_axis=0, concat_axis=0, tiled=True)
    expert_rows = arrived.reshape(experts * capacity, D)
    gate_val = jnp.dot(expert_rows, gate_weight[0], preferred_element_type=jnp.float32)
    up_val = jnp.dot(expert_rows, up_weight[0], preferred_element_type=jnp.float32)
    hidden_units = (gate_val * jax.nn.sigmoid(1.702 * gate_val) * (up_val + 1.0)).astype(
        jnp.bfloat16
    )
    down_local = down_weight[0]
    feature_cols = down_local.shape[1]
    hidden_full = lax.all_gather(hidden_units, "ffn", axis=1, tiled=True)
    expert_output = jnp.dot(hidden_full, down_local, preferred_element_type=jnp.float32)
    expert_output = expert_output.astype(jnp.bfloat16).reshape(
        lax.axis_size("seq"), capacity, feature_cols
    )
    returned = lax.all_to_all(expert_output, "seq", split_axis=0, concat_axis=0, tiled=True)
    returned = returned.reshape(experts * capacity, feature_cols)
    mixture = jnp.dot(combining, returned, preferred_element_type=jnp.float32)
    layer_output = (updated + mixture).astype(jnp.bfloat16)
    output_grad = lax.dot_general(
        combining, cotangent, row_contract, preferred_element_type=jnp.float32
    )
    output_grad = output_grad.astype(jnp.bfloat16).reshape(experts, capacity, feature_cols)
    grad_arrived = lax.all_to_all(output_grad, "seq", split_axis=0, concat_axis=0, tiled=True)
    grad_arrived = grad_arrived.reshape(experts * capacity, feature_cols)
    grad_local = lax.dot_general(
        hidden_full, grad_arrived, row_contract, preferred_element_type=jnp.float32
    )
    return (layer_output, grad_local.astype(jnp.bfloat16)[None])


def solution(mesh):
    return jax.shard_map(
        body,
        mesh=mesh,
        in_specs=(
            P("seq", "ffn"),
            P("seq", "ffn"),
            P("seq", "ffn"),
            P("ffn"),
            P("ffn", "seq"),
            P("seq", "ffn"),
            P("ffn"),
            P("ffn", None),
            P("seq", None),
            P("seq", None, "ffn"),
            P("seq", None, "ffn"),
            P("seq", None, "ffn"),
            P("seq", "ffn"),
        ),
        out_specs=(P("seq", "ffn"), P("seq", None, "ffn")),
        check_vma=False,
    )
```

profile of v0, /device:TPU:16, one launch (start us, length us, event | category | flops | bytes accessed | tf_op | source)
XLA Modules:
  0.0 499.3 jit_solution(5799736612471988416)
XLA Ops:
  8.0 4.3 collective-permute-start.1
  12.2 4.3 collective-permute-start
  16.7 1.0 copy.59
  17.8 3.0 collective-permute-done.1
  20.7 1.0 fusion.38
  23.4 1.0 convolution_convert_fusion.5
  24.4 76.6 %all-gather.5.cloned.1.call-done = bf16[64,45,512]{2,1,0:T(8,128)(2,1)} async-done(((bf16[1,45,512]{2,1,0:T(8,128)(2,1)}), bf16[64,45,512]{2,1,0:T(8,128)(2,1)}) %all-gather.5.cloned.1.call-update) | async-done | bytes 2949136 | tf_op jit(solution)/shard_map/all_gather | solution.py:69
  101.0 4.6 reshape.149
  105.6 3.9 fusion.39
  110.1 34.4 %reduce-scatter.4.cloned.1.call-done = f32[128,360]{0,1:T(8,128)} async-done(((f32[128,2880]{0,1:T(8,128)}), f32[128,360]{0,1:T(8,128)}) %reduce-scatter.4.cloned.1.call-update) | async-done | bytes 184336
  144.5 1.0 multiply_reduce_fusion
  145.5 12.9 %psum.14 = f32[128]{0:T(128)S(1)} all-reduce(f32[128]{0:T(128)S(1)} %multiply_reduce_fusion), channel_id=1, replica_groups=mesh['seq'=64,'ffn'=8] {'ffn'}, use_global_device_ids=true, to_apply=%region_6.7 | all-reduce | flops 128 | bytes 1024 | tf_op jit(solution)/shard_map/psum | solution.py:77
  158.4 1.0 fusion.16
  159.5 13.3 %all_gather.10 = bf16[128,2880]{0,1:T(8,128)(2,1)S(1)} all-gather(bf16[128,360]{0,1:T(8,128)(2,1)S(1)} %fusion.16), channel_id=1, replica_groups=mesh['seq'=64,'ffn'=8] {'ffn'}, dimensions={1}, use_global_device_ids=true | all-gather | bytes 829440 | tf_op jit(solution)/shard_map/all_gather | solution.py:108
  172.8 1.2 fusion.17
  174.0 23.8 %psum.15 = f32[128,64]{0,1:T(8,128)S(1)} all-reduce(f32[128,64]{0,1:T(8,128)S(1)} %fusion.17), channel_id=1, replica_groups=mesh['seq'=64,'ffn'=8] {'ffn'}, use_global_device_ids=true, to_apply=%region_7.8 | all-reduce | flops 8192 | bytes 65536 | tf_op jit(solution)/shard_map/psum | solution.py:81
  199.8 4.3 convolution_convert_fusion
  204.1 8.5 %copy.68 = bf16[1024,2880]{1,0:T(8,128)(2,1)} copy(bf16[1024,2880]{0,1:T(8,128)(2,1)} %convolution_convert_fusion) | data formatting | bytes 11796480 | tf_op jit(solution)/shard_map/convert_element_type | solution.py:112
  212.6 147.3 %all_to_all.15 = bf16[64,16,2880]{2,1,0:T(8,128)(2,1)S(1)} all-to-all(bf16[64,16,2880]{2,1,0:T(8,128)(2,1)} %bitcast.71), channel_id=1, replica_groups=mesh['seq'=64,'ffn'=8] {'seq'}, dimensions={0} | all-to-all | bytes 11796480 | tf_op jit(solution)/shard_map/all_to_all | solution.py:113
  359.9 2.2 fusion.10
  362.1 3.0 fusion.5
  365.4 1.3 fusion.15
  367.7 1.2 copy.70
  368.9 15.8 %all-to-all-start.2 = ((bf16[64,16,360]{2,1,0:T(8,128)(2,1)}), bf16[64,16,360]{2,1,0:T(8,128)(2,1)S(1)}, u32[]{:S(2)}, u32[]{:S(2)}) async-start(bf16[64,16,360]{2,1,0:T(8,128)(2,1)} %bitcast.22), calls=%async_computation.2 | async-start | bytes 1572864 | tf_op jit(solution)/shard_map/all_to_all | solution.py:135
  384.7 59.6 %all-gather.7.cloned.1.call-done = bf16[8,180,1024]{2,1,0:T(8,128)(2,1)} async-done(((bf16[1,180,1024]{2,1,0:T(8,128)(2,1)}), bf16[8,180,1024]{2,1,0:T(8,128)(2,1)}) %all-gather.7.cloned.1.call-update) | async-done | bytes 2949136 | tf_op jit(solution)/shard_map/all_gather | solution.py:122
  444.3 4.3 reshape.151
  448.6 3.2 convolution_convert_fusion.3
  451.8 1.2 copy.69
  453.0 13.4 %all-to-all-start.1 = ((bf16[64,16,360]{2,1,0:T(8,128)(2,1)}), bf16[64,16,360]{2,1,0:T(8,128)(2,1)S(1)}, u32[]{:S(2)}, u32[]{:S(2)}) async-start(bf16[64,16,360]{2,1,0:T(8,128)(2,1)} %bitcast.19), calls=%async_computation.1 | async-start | bytes 1572864 | tf_op jit(solution)/shard_map/all_to_all | solution.py:127
  466.3 4.6 fusion
  470.9 20.8 %all-to-all-done.1 = bf16[64,16,360]{2,1,0:T(8,128)(2,1)S(1)} async-done(((bf16[64,16,360]{2,1,0:T(8,128)(2,1)}), bf16[64,16,360]{2,1,0:T(8,128)(2,1)S(1)}, u32[]{:S(2)}, u32[]{:S(2)}) %all-to-all-start.1) | async-done | bytes 737312 | tf_op jit(solution)/shard_map/all_to_all | solution.py:127
  491.7 1.1 fusion.7
  (49 shorter events, 6.5 us)
Async XLA Ops:
  7.2 441.4 %copy-start = (bf16[1,1440,360]{2,1,0:T(8,128)(2,1)S(1)}, bf16[1,1440,360]{2,1,0:T(8,128)(2,1)}, u32[]{:S(2)}) copy-start(bf16[1,1440,360]{2,1,0:T(8,128)(2,1)} %param.24) | copy-start | bytes 3110404
  7.2 93.8 %all-gather.5.cloned.1.call-start = ((), (), s32[]{:S(2)}) async-start(), calls=%async_computation.4 | async-start | bytes 3194880 | tf_op jit(solution)/shard_map/all_gather | solution.py:69
  7.9 136.6 %reduce-scatter.4.cloned.1.call-start = ((), (), s32[]{:S(2)}) async-start(), calls=%async_computation.6 | async-start | bytes 1658880
  8.0 12.8 %collective-permute-start.1 = (bf16[128,64]{0,1:T(8,128)(2,1)}, bf16[128,64]{0,1:T(8,128)(2,1)S(1)}, u32[]{:S(2)}, u32[]{:S(2)}) collective-permute-start(bf16[128,64]{0,1:T(8,128)(2,1)} %param.14), channel_id=1, source_target_pairs={{0,8},{8,16},{16,24},{24,32},{32,40},{40,48},{48,56},{56,64},{64,7... | collective-permute-start | bytes 49160 | tf_op jit(solution)/shard_map/ppermute | solution.py:17
  12.2 11.1 %collective-permute-start = (bf16[128,64]{0,1:T(8,128)(2,1)}, bf16[128,64]{0,1:T(8,128)(2,1)S(1)}, u32[]{:S(2)}, u32[]{:S(2)}) collective-permute-start(bf16[128,64]{0,1:T(8,128)(2,1)} %param.15), channel_id=1, source_target_pairs={{0,8},{8,16},{16,24},{24,32},{32,40},{40,48},{48,56},{56,64},{64,7... | collective-permute-start | bytes 49160 | tf_op jit(solution)/shard_map/ppermute | solution.py:17
  105.6 4.0 copy-start.6
  105.6 38.9 %copy-start.2 = (bf16[128,360]{0,1:T(8,128)(2,1)S(1)}, bf16[128,360]{0,1:T(8,128)(2,1)}, u32[]{:S(2)}) copy-start(bf16[128,360]{0,1:T(8,128)(2,1)} %param.18) | copy-start | bytes 276484
  105.6 52.9 %copy-start.5 = (f32[360]{0:T(512)S(1)}, f32[360]{0:T(512)}, u32[]{:S(2)}) copy-start(f32[360]{0:T(512)} %param.19) | copy-start | bytes 4324
  109.5 63.3 %copy-start.4 = (bf16[360,64]{0,1:T(8,128)(2,1)S(1)}, bf16[360,64]{0,1:T(8,128)(2,1)}, u32[]{:S(2)}) copy-start(bf16[360,64]{0,1:T(8,128)(2,1)} %param.20) | copy-start | bytes 138244
  109.5 334.7 %all-gather.7.cloned.1.call-start = ((), (), s32[]{:S(2)}) async-start(), calls=%async_computation.5 | async-start | bytes 3391488 | tf_op jit(solution)/shard_map/all_gather | solution.py:122
  212.6 147.3 %copy-start.7 = (bf16[1,2880,180]{1,2,0:T(8,128)(2,1)S(1)}, bf16[1,2880,180]{1,2,0:T(8,128)(2,1)}, u32[]{:S(2)}) copy-start(bf16[1,2880,180]{1,2,0:T(8,128)(2,1)} %param.22) | copy-start | bytes 3110404
  359.9 2.2 copy-start.8
  365.0 2.3 copy-start.3
  368.9 84.1 %all-to-all-start.2 = ((bf16[64,16,360]{2,1,0:T(8,128)(2,1)}), bf16[64,16,360]{2,1,0:T(8,128)(2,1)S(1)}, u32[]{:S(2)}, u32[]{:S(2)}) async-start(bf16[64,16,360]{2,1,0:T(8,128)(2,1)} %bitcast.22), calls=%async_computation.2 | async-start | bytes 1572864 | tf_op jit(solution)/shard_map/all_to_all | solution.py:135
  453.0 38.7 %all-to-all-start.1 = ((bf16[64,16,360]{2,1,0:T(8,128)(2,1)}), bf16[64,16,360]{2,1,0:T(8,128)(2,1)S(1)}, u32[]{:S(2)}, u32[]{:S(2)}) async-start(bf16[64,16,360]{2,1,0:T(8,128)(2,1)} %bitcast.19), calls=%async_computation.1 | async-start | bytes 1572864 | tf_op jit(solution)/shard_map/all_to_all | solution.py:127
  466.3 25.3 %copy-start.1 = (f32[128,360]{0,1:T(8,128)S(1)}, f32[128,360]{0,1:T(8,128)}, u32[]{:S(2)}) copy-start(f32[128,360]{0,1:T(8,128)} %reduce-scatter.4.cloned.1.call-done) | copy-start | bytes 552964
Sparse Core Ops, SparseCore 0:
  11.1 89.8 all-gather.4
  109.6 34.8 reduce-scatter.3
  365.2 79.0 all-gather.6
where the time goes:
time: 500 us; the launch traced here: 499 us
  blocking collectives  197 us (39%)
  waiting for transfers between devices  195 us (39%)
  starting transfers between devices  37.8 us (8%)
  matrix products  28.1 us (6%)
  local copies, waits for them, and re-layouts  22.4 us (4%)
  between operations  14 us (3%)
    all_to_all x1, blocking collectives, body(): lax.all_to_all(local_slots, 'seq', split_axis=0, concat_axis=0, tiled=True)  147 us
    all_gather x1, waiting for transfers between devices, body(): lax.all_gather(out_weight, 'seq', axis=1, tiled=True)  76.6 us
    all_gather x1, waiting for transfers between devices, body(): hidden_full = lax.all_gather(hidden_units, 'ffn', axis=1, tiled=True)  59.6 us
    unnamed x4, waiting for transfers between devices  35.1 us
    psum x1, blocking collectives, body(): lax.psum(jnp.dot(normed, router_f32, precision=lax.Precision.HIGHEST), 'f...  23.8 us
    all_to_all x1, waiting for transfers between devices, body(): lax.all_to_all(expert_output, 'seq', split_axis=0, concat_axis=0, tiled=T...  20.8 us
    all_to_all x1, starting transfers between devices, body(): lax.all_to_all(output_grad, 'seq', split_axis=0, concat_axis=0, tiled=True)  15.8 us
    all_to_all x1, starting transfers between devices, body(): lax.all_to_all(expert_output, 'seq', split_axis=0, concat_axis=0, tiled=T...  13.4 us
  transfers between devices with their start and end apart: 7, of which 5 were waited for; matrix products, arithmetic and copies ran while one was open for 4% of the time, Pallas kernels for 0%

commit v1 on v0

v1 whole, which is shorter than its diff:
```python
import math

import jax
import jax.numpy as jnp
from jax import lax
from jax.sharding import Mesh, PartitionSpec as P

D = 2880
QUERY_HEADS = 64
KEY_VALUE_HEADS = 8
HEAD_SIZE = 64
VISIBLE_TOKENS = 128
TOPK = 4

SEQ = ("y", "z")
ROW_CONTRACT = (((0,), (0,)), ((), ()))


def from_previous_block(value):
    count = lax.axis_size("y") * lax.axis_size("z")
    return lax.ppermute(value, SEQ, [(source, source + 1) for source in range(count - 1)])


def swap_y_and_f(value):
    side, depth = lax.axis_size("y"), lax.axis_size("z")
    pairs = [
        ((y * depth + z) * side + f, (f * depth + z) * side + y)
        for y in range(side)
        for z in range(depth)
        for f in range(side)
    ]
    return lax.ppermute(value, ("y", "z", "f"), pairs)


def to_all(value, axis):
    copies = jnp.broadcast_to(value[None], (lax.axis_size(axis), *value.shape))
    return lax.all_to_all(copies, axis, split_axis=0, concat_axis=0, tiled=True)


def attend(queries, key_vectors, head_value_vectors, head_sink_logits):
    tok_rows = queries.shape[0]
    key_heads = key_vectors.shape[1] // HEAD_SIZE
    query_grouping = QUERY_HEADS // KEY_VALUE_HEADS
    prev_keys, prev_values = from_previous_block((key_vectors, head_value_vectors))
    all_keys = jnp.concatenate([prev_keys, key_vectors], axis=0).reshape(
        2 * tok_rows, key_heads, HEAD_SIZE
    )
    all_values = jnp.concatenate([prev_values, head_value_vectors], axis=0).reshape(
        2 * tok_rows, key_heads, HEAD_SIZE
    )
    query_heads = queries.reshape(tok_rows, key_heads, query_grouping, HEAD_SIZE)
    scores = jnp.einsum(
        "tkgd,skd->kgts", query_heads, all_keys, preferred_element_type=jnp.float32
    ) * HEAD_SIZE ** (-0.5)
    offset = lax.axis_index(SEQ) * tok_rows
    query_pos = offset + jnp.arange(tok_rows, dtype=jnp.int32)
    key_pos = offset - tok_rows + jnp.arange(2 * tok_rows, dtype=jnp.int32)
    valid = (
        (key_pos[None, :] >= 0)
        & (key_pos[None, :] <= query_pos[:, None])
        & (key_pos[None, :] > query_pos[:, None] - VISIBLE_TOKENS)
    )
    scores = jnp.where(valid, scores, -1e30)
    sink_entries = head_sink_logits.reshape(key_heads, query_grouping)[:, :, None]
    highest = jnp.maximum(jnp.max(scores, axis=-1), sink_entries)
    powers = jnp.exp(scores - highest[..., None])
    denom = jnp.sum(powers, axis=-1) + jnp.exp(sink_entries - highest)
    weights = (powers / denom[..., None]).astype(jnp.bfloat16)
    attended = jnp.einsum("kgts,skd->tkgd", weights, all_values, preferred_element_type=jnp.float32)
    return attended.astype(jnp.bfloat16).reshape(tok_rows, key_heads * query_grouping * HEAD_SIZE)


def slots_of(ids, experts, capacity):
    tok_rows = ids.shape[0]
    onehot = (ids[:, :, None] == jnp.arange(experts, dtype=jnp.int32)).astype(jnp.float32)
    counts = jnp.sum(onehot, axis=1)
    row_index = jnp.arange(tok_rows, dtype=jnp.int32)
    strictly_lower = (row_index[:, None] > row_index[None, :]).astype(jnp.bfloat16)
    before = jnp.dot(
        strictly_lower, counts.astype(jnp.bfloat16), preferred_element_type=jnp.float32
    )
    slot = jnp.sum(onehot * before[:, None, :], axis=-1)
    slot_hot = (
        slot[:, :, None] == jnp.arange(capacity, dtype=jnp.int32).astype(jnp.float32)
    ).astype(jnp.float32)
    return onehot, slot_hot


def body(
    queries,
    key_vectors,
    head_value_vectors,
    head_sink_logits,
    out_weight,
    residual,
    norm_gain,
    router_weight,
    expert_ids,
    gate_weight,
    up_weight,
    down_weight,
    cotangent,
):
    tok_rows, chunk = residual.shape
    side, depth = lax.axis_size("y"), lax.axis_size("z")
    experts = router_weight.shape[1]
    capacity = 2 * TOPK * tok_rows // experts
    hidden_part = gate_weight.shape[2]

    both = jnp.concatenate([gate_weight[0].T, up_weight[0].T], axis=0)
    both_full = lax.all_gather(both, "f", axis=0, tiled=True)

    out_columns = to_all(out_weight.T, "z").reshape(chunk, out_weight.shape[0])
    attended = attend(queries, key_vectors, head_value_vectors, head_sink_logits)
    attended_all = to_all(attended, "y").reshape(side * tok_rows, attended.shape[1])
    residual_here = swap_y_and_f(residual)
    gain_here = swap_y_and_f(norm_gain)
    ids_here = swap_y_and_f(expert_ids)

    partial_out = lax.dot_general(
        attended_all, out_columns, (((1,), (1,)), ((), ())), preferred_element_type=jnp.float32
    )
    partial_out = partial_out.astype(jnp.bfloat16).reshape(side, tok_rows, chunk)
    parts = lax.all_to_all(partial_out, "f", split_axis=0, concat_axis=0, tiled=True)
    updated_here = residual_here.astype(jnp.float32) + jnp.sum(parts.astype(jnp.float32), axis=0)
    squares = jnp.sum(updated_here * updated_here, axis=-1, keepdims=True)
    squares_high = squares.astype(jnp.bfloat16)
    squares_low = (squares - squares_high.astype(jnp.float32)).astype(jnp.bfloat16)
    rows_here = jnp.concatenate(
        [(updated_here * gain_here).astype(jnp.bfloat16), squares_high, squares_low], axis=1
    )
    onehot_here, slot_hot_here = slots_of(ids_here, experts, capacity)
    placing = (
        jnp.einsum("tje,tjc->tec", onehot_here, slot_hot_here)
        .reshape(tok_rows, experts * capacity)
        .astype(jnp.bfloat16)
    )
    local_slots = lax.dot_general(
        placing, rows_here, ROW_CONTRACT, preferred_element_type=jnp.float32
    )
    local_slots = local_slots.astype(jnp.bfloat16).reshape(experts, capacity, chunk + 2)
    arrived = lax.all_to_all(local_slots, SEQ, split_axis=0, concat_axis=0, tiled=True)

    updated = swap_y_and_f(updated_here)
    gained = updated * norm_gain
    logits_part = jnp.dot(gained, router_weight.astype(jnp.float32), precision=lax.Precision.HIGHEST)
    square_part = jnp.sum(updated * updated, axis=-1, keepdims=True)
    sums = jnp.sum(
        lax.all_gather(jnp.concatenate([logits_part, square_part], axis=1).T, "f", axis=0), axis=0
    ).T
    router_logits = sums[:, :experts] * lax.rsqrt(sums[:, experts:] / D + 1e-05)
    onehot, slot_hot = slots_of(expert_ids, experts, capacity)
    chosen = jnp.sum(onehot * router_logits[:, None, :], axis=-1)
    top_val = jnp.max(chosen, axis=-1, keepdims=True)
    gate_pow = jnp.exp(chosen - top_val)
    gates = (gate_pow / jnp.sum(gate_pow, axis=-1, keepdims=True)).astype(jnp.bfloat16)
    combining = (
        jnp.einsum("tj,tje,tjc->tec", gates.astype(jnp.float32), onehot, slot_hot)
        .reshape(tok_rows, experts * capacity)
        .astype(jnp.bfloat16)
    )
    output_grad = lax.dot_general(
        combining, cotangent, ROW_CONTRACT, preferred_element_type=jnp.float32
    )
    output_grad = output_grad.astype(jnp.bfloat16).reshape(experts, capacity, chunk)
    grad_arrived = lax.all_to_all(output_grad, SEQ, split_axis=0, concat_axis=0, tiled=True)
    grad_arrived = grad_arrived.reshape(experts * capacity, chunk)

    arrived = jnp.transpose(
        arrived.reshape(side, depth * capacity, chunk + 2), (1, 0, 2)
    )
    expert_rows = arrived[:, :, :chunk].reshape(depth * capacity, D)
    row_squares = jnp.sum(arrived[:, :, chunk:].astype(jnp.float32), axis=(1, 2))
    scaling = lax.rsqrt(row_squares / D + 1e-05)
    products = lax.dot_general(
        both_full, expert_rows, (((1,), (1,)), ((), ())), preferred_element_type=jnp.float32
    )
    products = (products * scaling).reshape(side, 2, hidden_part, depth * capacity)
    gate_val, up_val = products[:, 0], products[:, 1]
    hidden_units = (gate_val * jax.nn.sigmoid(1.702 * gate_val) * (up_val + 1.0)).astype(
        jnp.bfloat16
    )
    hidden_units = hidden_units.reshape(side * hidden_part, depth * capacity).T
    hidden_full = lax.all_gather(hidden_units, "f", axis=0, tiled=True)

    expert_output = jnp.dot(hidden_full, down_weight[0], preferred_element_type=jnp.float32)
    expert_output = expert_output.astype(jnp.bfloat16).reshape(experts, capacity, chunk)
    returned = lax.all_to_all(expert_output, SEQ, split_axis=0, concat_axis=0, tiled=True)
    returned = returned.reshape(experts * capacity, chunk)
    mixture = jnp.dot(combining, returned, preferred_element_type=jnp.float32)
    layer_output = (updated + mixture).astype(jnp.bfloat16)
    grad_local = lax.dot_general(
        hidden_full, grad_arrived, ROW_CONTRACT, preferred_element_type=jnp.float32
    )
    return (layer_output, grad_local.astype(jnp.bfloat16)[None])


def solution(mesh):
    seq, ffn = mesh.devices.shape
    side = math.isqrt(seq)
    grid = Mesh(mesh.devices.reshape(side, seq // side, ffn), ("y", "z", "f"))
    return jax.shard_map(
        body,
        mesh=grid,
        in_specs=(
            P(SEQ, "f"),
            P(SEQ, "f"),
            P(SEQ, "f"),
            P("f"),
            P("f", SEQ),
            P(SEQ, "f"),
            P("f"),
            P("f", None),
            P(SEQ, None),
            P(SEQ, None, "f"),
            P(SEQ, None, "f"),
            P(SEQ, None, "f"),
            P(SEQ, "f"),
        ),
        out_specs=(P(SEQ, "f"), P(SEQ, None, "f")),
        check_vma=False,
    )
```

time: 500 us -> 262 us (0.52)
  blocking collectives: 197 us -> 44.7 us
  waiting for transfers between devices: 195 us -> 101 us
  starting transfers between devices: 37.8 us -> 58.7 us
  local copies, waits for them, and re-layouts: 22.4 us -> 11.3 us
  matrix products: 28.1 us -> 23.1 us
    all_gather x2, waiting for transfers between devices: 136 us -> 0.04 us  [the longest x1 0.02 us: body(): hidden_full = lax.all_gather(hidden_units, 'f', axis=0, tiled=True)]
    all_to_all x1, blocking collectives: 147 us -> 30.7 us  [body(): lax.all_to_all(local_slots, SEQ, split_axis=0, concat_axis=0, tiled=True)]
    all_to_all x2 -> x5, waiting for transfers between devices: 20.8 us -> 73.2 us  [the longest x1 21 us: body(): lax.all_to_all(output_grad, SEQ, split_axis=0, concat_axis=0, tiled=True)]
    psum x2 -> x0, blocking collectives: 36.7 us -> none  [the longest x1 23.8 us: body(): lax.psum(jnp.dot(normed, router_f32, precision=lax.Precision.HIGHEST), 'f...]
    unnamed x4 -> x2, waiting for transfers between devices: 35.1 us -> 0.03 us
    ppermute x2 -> x6, waiting for transfers between devices: 2.96 us -> 27.9 us  [the longest x4 27.9 us: swap_y_and_f(): return lax.ppermute(value, ('y', 'z', 'f'), pairs)]
    ppermute x2 -> x6, starting transfers between devices: 8.57 us -> 21.1 us  [the longest x4 12.4 us: swap_y_and_f(): return lax.ppermute(value, ('y', 'z', 'f'), pairs)]
    unnamed x22 -> x30, local copies, waits for them, and re-layouts: 10.1 us -> 0.98 us
  transfers between devices with their start and end apart: 7 -> 13, of which waited for: 5 -> 7; matrix products, arithmetic and copies ran while one was open for 4% -> 9% of each run, Pallas kernels for 0% -> 0%
where the time goes in v1:
time: 262 us; the launch traced here: 261 us
  waiting for transfers between devices  101 us (39%)
  starting transfers between devices  58.7 us (22%)
  blocking collectives  44.7 us (17%)
  matrix products  23.1 us (9%)
  between operations  14.5 us (6%)
  local copies, waits for them, and re-layouts  11.3 us (4%)
  other arithmetic  7.84 us (3%)
    all_to_all x1, blocking collectives, body(): lax.all_to_all(local_slots, SEQ, split_axis=0, concat_axis=0, tiled=True)  30.7 us
    ppermute x4, waiting for transfers between devices, swap_y_and_f(): return lax.ppermute(value, ('y', 'z', 'f'), pairs)  27.9 us
    all_to_all x1, waiting for transfers between devices, body(): lax.all_to_all(output_grad, SEQ, split_axis=0, concat_axis=0, tiled=True)  21 us
    all_to_all x1, waiting for transfers between devices, body(): lax.all_to_all(expert_output, SEQ, split_axis=0, concat_axis=0, tiled=True)  20.2 us
    all_to_all x1, waiting for transfers between devices, body(): lax.all_to_all(partial_out, 'f', split_axis=0, concat_axis=0, tiled=True)  18.6 us
    all_to_all x2, starting transfers between devices, to_all(): return lax.all_to_all(copies, axis, split_axis=0, concat_axis=0, tiled=True)  15.9 us
    all_gather x1, blocking collectives, body(): lax.all_gather(jnp.concatenate([logits_part, square_part], axis=1).T, 'f'...  14 us
    all_to_all x2, waiting for transfers between devices, to_all(): return lax.all_to_all(copies, axis, split_axis=0, concat_axis=0, tiled=True)  13.4 us
  transfers between devices with their start and end apart: 13, of which 7 were waited for; matrix products, arithmetic and copies ran while one was open for 9% of the time, Pallas kernels for 0%

profile of v1, /device:TPU:16, one launch (start us, length us, event | category | flops | bytes accessed | tf_op | source)
XLA Modules:
  0.0 261.4 jit_solution(10488848741737030400)
XLA Ops:
  7.2 3.3 %pad_maximum_fusion = bf16[360,2880]{1,0:T(8,128)(2,1)} fusion(bf16[180,2880]{1,0:T(8,128)(2,1)} %bitcast.96, bf16[180,2880]{1,0:T(8,128)(2,1)} %bitcast.97), kind=kLoop, calls=%fused_computation.3 | loop fusion | flops 4147200 | bytes 4147200 | tf_op jit(solution)/shard_map/concatenate | solution.py:110
  11.2 4.4 %collective-permute-start.2 = (bf16[128,64]{0,1:T(8,128)(2,1)S(1)}, bf16[128,64]{0,1:T(8,128)(2,1)S(1)}, u32[]{:S(2)}, u32[]{:S(2)}) collective-permute-start(bf16[128,64]{0,1:T(8,128)(2,1)S(1)} %copy-done.5), channel_id=1, source_target_pairs={{0,8},{8,16},{16,24},{24,32},{32,40},{40,48},{48,56},{56,64},{64,7... | collective-permute-start | bytes 49160 | tf_op jit(solution)/shard_map/ppermute | solution.py:21
  15.6 4.3 %collective-permute-start.1 = (bf16[128,64]{0,1:T(8,128)(2,1)S(1)}, bf16[128,64]{0,1:T(8,128)(2,1)S(1)}, u32[]{:S(2)}, u32[]{:S(2)}) collective-permute-start(bf16[128,64]{0,1:T(8,128)(2,1)S(1)} %copy-done.11), channel_id=1, source_target_pairs={{0,8},{8,16},{16,24},{24,32},{32,40},{40,48},{48,56},{56,64},{64,7... | collective-permute-start | bytes 49160 | tf_op jit(solution)/shard_map/ppermute | solution.py:21
  20.7 8.5 %all-to-all-start.1 = ((bf16[8,45,512]{2,1,0:T(8,128)(2,1)}), bf16[8,45,512]{2,1,0:T(8,128)(2,1)S(1)}, u32[]{:S(2)}, u32[]{:S(2)}) async-start(bf16[8,45,512]{2,1,0:T(8,128)(2,1)} %broadcast_in_dim.22), calls=%async_computation.1 | async-start | bytes 786432 | tf_op jit(solution)/shard_map/all_to_all | solution.py:37
  30.7 12.7 %all-to-all-done.1 = bf16[8,45,512]{2,1,0:T(8,128)(2,1)S(1)} async-done(((bf16[8,45,512]{2,1,0:T(8,128)(2,1)}), bf16[8,45,512]{2,1,0:T(8,128)(2,1)S(1)}, u32[]{:S(2)}, u32[]{:S(2)}) %all-to-all-start.1) | async-done | bytes 368672 | tf_op jit(solution)/shard_map/all_to_all | solution.py:37
  43.3 1.1 broadcast_in_dim.21
  44.4 7.4 %all-to-all-start = ((bf16[8,128,512]{2,1,0:T(8,128)(2,1)}), bf16[8,128,512]{2,1,0:T(8,128)(2,1)S(1)}, u32[]{:S(2)}, u32[]{:S(2)}) async-start(bf16[8,128,512]{2,1,0:T(8,128)(2,1)} %broadcast_in_dim.21), calls=%async_computation | async-start | bytes 2097152 | tf_op jit(solution)/shard_map/all_to_all | solution.py:37
  51.8 2.8 %collective-permute-start.5 = (f32[360]{0:T(512)S(1)}, f32[360]{0:T(512)S(1)}, u32[]{:S(2)}, u32[]{:S(2)}) collective-permute-start(f32[360]{0:T(512)S(1)} %copy-done.6), channel_id=1, source_target_pairs={{0,0},{1,64},{2,128},{3,192},{4,256},{5,320},{6,384},{7,448},{8,8}... | collective-permute-start | bytes 4328 | tf_op jit(solution)/shard_map/ppermute | solution.py:32
  54.7 4.8 %collective-permute-start = (bf16[128,360]{0,1:T(8,128)(2,1)S(1)}, bf16[128,360]{0,1:T(8,128)(2,1)S(1)}, u32[]{:S(2)}, u32[]{:S(2)}) collective-permute-start(bf16[128,360]{0,1:T(8,128)(2,1)S(1)} %copy-done.10), channel_id=1, source_target_pairs={{0,0},{1,64},{2,128},{3,192},{4,256},{5,320},{6,384},{7,448},{8,8}... | collective-permute-start | bytes 276488 | tf_op jit(solution)/shard_map/ppermute | solution.py:32
  59.5 2.9 %collective-permute-start.4 = (s32[128,4]{0,1:T(4,128)S(1)}, s32[128,4]{0,1:T(4,128)S(1)}, u32[]{:S(2)}, u32[]{:S(2)}) collective-permute-start(s32[128,4]{0,1:T(4,128)S(1)} %copy-done.7), channel_id=1, source_target_pairs={{0,0},{1,64},{2,128},{3,192},{4,256},{5,320},{6,384},{7,448},{8,8}... | collective-permute-start | bytes 6152 | tf_op jit(solution)/shard_map/ppermute | solution.py:32
  62.4 15.8 %collective-permute-done.4 = s32[128,4]{0,1:T(4,128)S(1)} collective-permute-done((s32[128,4]{0,1:T(4,128)S(1)}, s32[128,4]{0,1:T(4,128)S(1)}, u32[]{:S(2)}, u32[]{:S(2)}) %collective-permute-start.4) | collective-permute-done | bytes 2080 | tf_op jit(solution)/shard_map/ppermute | solution.py:32
  79.7 1.0 copy.94
  80.7 7.7 %all-to-all-start.2 = ((bf16[8,128,360]{1,2,0:T(8,128)(2,1)}), bf16[8,128,360]{1,2,0:T(8,128)(2,1)S(1)}, u32[]{:S(2)}, u32[]{:S(2)}) async-start(bf16[8,128,360]{1,2,0:T(8,128)(2,1)} %bitcast.89), calls=%async_computation.2 | async-start | bytes 1474560 | tf_op jit(solution)/shard_map/all_to_all | solution.py:124
  90.7 18.6 %all-to-all-done.2 = bf16[8,128,360]{1,2,0:T(8,128)(2,1)S(1)} async-done(((bf16[8,128,360]{1,2,0:T(8,128)(2,1)}), bf16[8,128,360]{1,2,0:T(8,128)(2,1)S(1)}, u32[]{:S(2)}, u32[]{:S(2)}) %all-to-all-start.2) | async-done | bytes 737312 | tf_op jit(solution)/shard_map/all_to_all | solution.py:124
  110.3 30.7 %all_to_all.30 = bf16[64,16,362]{2,1,0:T(8,128)(2,1)S(1)} all-to-all(bf16[64,16,362]{2,1,0:T(8,128)(2,1)S(1)} %bitcast.94), channel_id=1, replica_groups=mesh['y'=8,'z'=8,'f'=8] {'y','z'}, dimensions={0} | all-to-all | bytes 1482752 | tf_op jit(solution)/shard_map/all_to_all | solution.py:142
  141.6 9.7 %convolution_multiply_fusion = f32[2880,128]{1,0:T(8,128)} fusion(bf16[2880,2880]{1,0:T(8,128)(2,1)} %all-gather.5.cloned.1.call-done, bf16[128,2880]{0,1:T(8,128)(2,1)S(1)} %bitcast.100, f32[128]{0:T(128)S(1)} %add_rsqrt_fusion), kind=kOutput, calls=%fused_computation | convolution fusion | flops 2123735040 | bytes 18801152 | tf_op jit(solution)/shard_map/dot_general | solution.py:175
  151.3 1.4 reshape.199
  152.7 1.0 fusion.48
  153.7 1.2 add.91
  156.3 1.9 collective-permute-start.3
  158.4 12.2 %collective-permute-done.3 = f32[128,360]{0,1:T(8,128)S(1)} collective-permute-done((f32[128,360]{0,1:T(8,128)S(1)}, f32[128,360]{0,1:T(8,128)S(1)}, u32[]{:S(2)}, u32[]{:S(2)}) %collective-permute-start.3) | collective-permute-done | bytes 184352 | tf_op jit(solution)/shard_map/ppermute | solution.py:32
  170.9 14.0 %all-gather.1 = f32[8,65,128]{2,1,0:T(8,128)S(1)} all-gather(f32[1,65,128]{2,1,0:T(8,128)S(1)} %maximum_bitcast_fusion), channel_id=2, replica_groups=mesh['y'=8,'z'=8,'f'=8] {'f'}, dimensions={0}, use_global_device_ids=true | all-gather | bytes 299520 | tf_op jit(solution)/shard_map/all_gather | solution.py:149
  186.0 1.3 fusion.10
  188.3 1.2 copy.88
  189.5 8.5 %all-to-all-start.5 = ((bf16[64,16,360]{2,1,0:T(8,128)(2,1)}), bf16[64,16,360]{2,1,0:T(8,128)(2,1)S(1)}, u32[]{:S(2)}, u32[]{:S(2)}) async-start(bf16[64,16,360]{2,1,0:T(8,128)(2,1)} %bitcast.32), calls=%async_computation.5 | async-start | bytes 1572864 | tf_op jit(solution)/shard_map/all_to_all | solution.py:166
  198.0 3.2 %convolution_convert_fusion.3 = bf16[1024,360]{0,1:T(8,128)(2,1)S(1)} fusion(bf16[1024,1440]{0,1:T(8,128)(2,1)} %all-gather.7.cloned.1.call-done, bf16[1,1440,360]{2,1,0:T(8,128)(2,1)S(1)} %copy-done), kind=kOutput, calls=%fused_computation.7 | convolution fusion | flops 1062051840 | bytes 4723200 | tf_op jit(solution)/shard_map/dot_general | solution.py:186
  201.2 1.2 copy.87
  202.4 21.0 %all-to-all-done.5 = bf16[64,16,360]{2,1,0:T(8,128)(2,1)S(1)} async-done(((bf16[64,16,360]{2,1,0:T(8,128)(2,1)}), bf16[64,16,360]{2,1,0:T(8,128)(2,1)S(1)}, u32[]{:S(2)}, u32[]{:S(2)}) %all-to-all-start.5) | async-done | bytes 737312 | tf_op jit(solution)/shard_map/all_to_all | solution.py:166
  223.4 5.4 %all-to-all-start.4 = ((bf16[64,16,360]{2,1,0:T(8,128)(2,1)}), bf16[64,16,360]{2,1,0:T(8,128)(2,1)S(1)}, u32[]{:S(2)}, u32[]{:S(2)}) async-start(bf16[64,16,360]{2,1,0:T(8,128)(2,1)} %bitcast.29), calls=%async_computation.4 | async-start | bytes 1572864 | tf_op jit(solution)/shard_map/all_to_all | solution.py:188
  228.8 4.5 %fusion = bf16[1,1440,360]{2,1,0:T(8,128)(2,1)} fusion(bf16[1024,1440]{0,1:T(8,128)(2,1)} %all-gather.7.cloned.1.call-done, bf16[1024,360]{1,0:T(8,128)(2,1)S(1)} %bitcast.99), kind=kOutput, calls=%fused_computation.2 | convolution fusion | flops 1062201600 | bytes 4723200 | tf_op jit(solution)/shard_map/dot_general | solution.py:192
  233.3 20.2 %all-to-all-done.4 = bf16[64,16,360]{2,1,0:T(8,128)(2,1)S(1)} async-done(((bf16[64,16,360]{2,1,0:T(8,128)(2,1)}), bf16[64,16,360]{2,1,0:T(8,128)(2,1)S(1)}, u32[]{:S(2)}, u32[]{:S(2)}) %all-to-all-start.4) | async-done | bytes 737312 | tf_op jit(solution)/shard_map/all_to_all | solution.py:188
  253.5 1.1 fusion.5
  (90 shorter events, 12.2 us)
Async XLA Ops:
  7.2 190.8 %copy-start = (bf16[1,1440,360]{2,1,0:T(8,128)(2,1)S(1)}, bf16[1,1440,360]{2,1,0:T(8,128)(2,1)}, u32[]{:S(2)}) copy-start(bf16[1,1440,360]{2,1,0:T(8,128)(2,1)} %param.24) | copy-start | bytes 3110404
  7.2 134.4 %all-gather.5.cloned.1.call-start = ((), (), s32[]{:S(2)}) async-start(), calls=%async_computation.6 | async-start | bytes 19077120 | tf_op jit(solution)/shard_map/all_gather | solution.py:111
  10.5 0.7 copy-start.5
  10.5 5.1 %copy-start.11 = (bf16[128,64]{0,1:T(8,128)(2,1)S(1)}, bf16[128,64]{0,1:T(8,128)(2,1)}, u32[]{:S(2)}) copy-start(bf16[128,64]{0,1:T(8,128)(2,1)} %param.15) | copy-start | bytes 49156
  10.5 9.4 %copy-start.3 = (bf16[512,45]{0,1:T(8,128)(2,1)S(1)}, bf16[512,45]{0,1:T(8,128)(2,1)}, u32[]{:S(2)}) copy-start(bf16[512,45]{0,1:T(8,128)(2,1)} %param.17) | copy-start | bytes 138244
  10.5 18.9 %copy-start.1 = (bf16[128,512]{1,0:T(8,128)(2,1)S(1)}, bf16[128,512]{1,0:T(8,128)(2,1)}, u32[]{:S(2)}) copy-start(bf16[128,512]{1,0:T(8,128)(2,1)} %param.13) | copy-start | bytes 393220
  11.2 18.7 %copy-start.9 = (f32[8]{0:T(128)S(1)}, f32[8]{0:T(128)}, u32[]{:S(2)}) copy-start(f32[8]{0:T(128)} %param.16) | copy-start | bytes 100
  11.2 18.3 %collective-permute-start.2 = (bf16[128,64]{0,1:T(8,128)(2,1)S(1)}, bf16[128,64]{0,1:T(8,128)(2,1)S(1)}, u32[]{:S(2)}, u32[]{:S(2)}) collective-permute-start(bf16[128,64]{0,1:T(8,128)(2,1)S(1)} %copy-done.5), channel_id=1, source_target_pairs={{0,8},{8,16},{16,24},{24,32},{32,40},{40,48},{48,56},{56,64},{64,7... | collective-permute-start | bytes 49160 | tf_op jit(solution)/shard_map/ppermute | solution.py:21
  15.6 14.6 %collective-permute-start.1 = (bf16[128,64]{0,1:T(8,128)(2,1)S(1)}, bf16[128,64]{0,1:T(8,128)(2,1)S(1)}, u32[]{:S(2)}, u32[]{:S(2)}) collective-permute-start(bf16[128,64]{0,1:T(8,128)(2,1)S(1)} %copy-done.11), channel_id=1, source_target_pairs={{0,8},{8,16},{16,24},{24,32},{32,40},{40,48},{48,56},{56,64},{64,7... | collective-permute-start | bytes 49160 | tf_op jit(solution)/shard_map/ppermute | solution.py:21
  20.7 22.6 %all-to-all-start.1 = ((bf16[8,45,512]{2,1,0:T(8,128)(2,1)}), bf16[8,45,512]{2,1,0:T(8,128)(2,1)S(1)}, u32[]{:S(2)}, u32[]{:S(2)}) async-start(bf16[8,45,512]{2,1,0:T(8,128)(2,1)} %broadcast_in_dim.22), calls=%async_computation.1 | async-start | bytes 786432 | tf_op jit(solution)/shard_map/all_to_all | solution.py:37
  30.6 21.2 %copy-start.6 = (f32[360]{0:T(512)S(1)}, f32[360]{0:T(512)}, u32[]{:S(2)}) copy-start(f32[360]{0:T(512)} %param.19) | copy-start | bytes 4324
  30.6 24.0 %copy-start.10 = (bf16[128,360]{0,1:T(8,128)(2,1)S(1)}, bf16[128,360]{0,1:T(8,128)(2,1)}, u32[]{:S(2)}) copy-start(bf16[128,360]{0,1:T(8,128)(2,1)} %param.18) | copy-start | bytes 276484
  30.6 28.8 %copy-start.7 = (s32[128,4]{0,1:T(4,128)S(1)}, s32[128,4]{0,1:T(4,128)}, u32[]{:S(2)}) copy-start(s32[128,4]{0,1:T(4,128)} %param.21) | copy-start | bytes 6148
  44.4 34.7 %all-to-all-start = ((bf16[8,128,512]{2,1,0:T(8,128)(2,1)}), bf16[8,128,512]{2,1,0:T(8,128)(2,1)S(1)}, u32[]{:S(2)}, u32[]{:S(2)}) async-start(bf16[8,128,512]{2,1,0:T(8,128)(2,1)} %broadcast_in_dim.21), calls=%async_computation | async-start | bytes 2097152 | tf_op jit(solution)/shard_map/all_to_all | solution.py:37
  51.8 57.5 %collective-permute-start.5 = (f32[360]{0:T(512)S(1)}, f32[360]{0:T(512)S(1)}, u32[]{:S(2)}, u32[]{:S(2)}) collective-permute-start(f32[360]{0:T(512)S(1)} %copy-done.6), channel_id=1, source_target_pairs={{0,0},{1,64},{2,128},{3,192},{4,256},{5,320},{6,384},{7,448},{8,8}... | collective-permute-start | bytes 4328 | tf_op jit(solution)/shard_map/ppermute | solution.py:32
  54.7 54.7 %collective-permute-start = (bf16[128,360]{0,1:T(8,128)(2,1)S(1)}, bf16[128,360]{0,1:T(8,128)(2,1)S(1)}, u32[]{:S(2)}, u32[]{:S(2)}) collective-permute-start(bf16[128,360]{0,1:T(8,128)(2,1)S(1)} %copy-done.10), channel_id=1, source_target_pairs={{0,0},{1,64},{2,128},{3,192},{4,256},{5,320},{6,384},{7,448},{8,8}... | collective-permute-start | bytes 276488 | tf_op jit(solution)/shard_map/ppermute | solution.py:32
  59.5 18.6 %collective-permute-start.4 = (s32[128,4]{0,1:T(4,128)S(1)}, s32[128,4]{0,1:T(4,128)S(1)}, u32[]{:S(2)}, u32[]{:S(2)}) collective-permute-start(s32[128,4]{0,1:T(4,128)S(1)} %copy-done.7), channel_id=1, source_target_pairs={{0,0},{1,64},{2,128},{3,192},{4,256},{5,320},{6,384},{7,448},{8,8}... | collective-permute-start | bytes 6152 | tf_op jit(solution)/shard_map/ppermute | solution.py:32
  62.4 26.9 %copy-start.12 = (f32[16]{0:T(128)}, f32[16]{0:T(128)S(1)}, u32[]{:S(2)}) copy-start(f32[16]{0:T(128)S(1)} %iota_convert_fusion) | copy-start | bytes 196
  80.7 28.6 %all-to-all-start.2 = ((bf16[8,128,360]{1,2,0:T(8,128)(2,1)}), bf16[8,128,360]{1,2,0:T(8,128)(2,1)S(1)}, u32[]{:S(2)}, u32[]{:S(2)}) async-start(bf16[8,128,360]{1,2,0:T(8,128)(2,1)} %bitcast.89), calls=%async_computation.2 | async-start | bytes 1474560 | tf_op jit(solution)/shard_map/all_to_all | solution.py:124
  88.4 109.6 %all-gather.7.cloned.1.call-start = ((), (), s32[]{:S(2)}) async-start(), calls=%async_computation.7 | async-start | bytes 3317760 | tf_op jit(solution)/shard_map/all_gather | solution.py:184
  154.8 1.1 copy-start.8
  154.9 15.7 %copy-start.4 = (bf16[360,64]{0,1:T(8,128)(2,1)S(1)}, bf16[360,64]{0,1:T(8,128)(2,1)}, u32[]{:S(2)}) copy-start(bf16[360,64]{0,1:T(8,128)(2,1)} %param.20) | copy-start | bytes 138244
  155.9 30.1 %copy-start.13 = (f32[16]{0:T(128)S(1)}, f32[16]{0:T(128)}, u32[]{:S(2)}) copy-start(f32[16]{0:T(128)} %copy-done.12) | copy-start | bytes 196
  156.3 14.2 %collective-permute-start.3 = (f32[128,360]{0,1:T(8,128)S(1)}, f32[128,360]{0,1:T(8,128)S(1)}, u32[]{:S(2)}, u32[]{:S(2)}) collective-permute-start(f32[128,360]{0,1:T(8,128)S(1)} %get-tuple-element.5), channel_id=1, source_target_pairs={{0,0},{1,64},{2,128},{3,192},{4,256},{5,320},{6,384},{7,448},{8,8}... | collective-permute-start | bytes 552968 | tf_op jit(solution)/shard_map/ppermute | solution.py:32
  186.0 1.9 copy-start.2
  189.5 33.9 %all-to-all-start.5 = ((bf16[64,16,360]{2,1,0:T(8,128)(2,1)}), bf16[64,16,360]{2,1,0:T(8,128)(2,1)S(1)}, u32[]{:S(2)}, u32[]{:S(2)}) async-start(bf16[64,16,360]{2,1,0:T(8,128)(2,1)} %bitcast.32), calls=%async_computation.5 | async-start | bytes 1572864 | tf_op jit(solution)/shard_map/all_to_all | solution.py:166
  223.4 30.1 %all-to-all-start.4 = ((bf16[64,16,360]{2,1,0:T(8,128)(2,1)}), bf16[64,16,360]{2,1,0:T(8,128)(2,1)S(1)}, u32[]{:S(2)}, u32[]{:S(2)}) async-start(bf16[64,16,360]{2,1,0:T(8,128)(2,1)} %bitcast.29), calls=%async_computation.4 | async-start | bytes 1572864 | tf_op jit(solution)/shard_map/all_to_all | solution.py:188
Sparse Core Ops, SparseCore 0:
  10.6 107.1 all-gather.4
  156.0 30.1 all-gather.6

commit v2 on v1

v2 whole, which is shorter than its diff:
```python
import functools
import math

import jax
import jax.numpy as jnp
from jax import lax
from jax.experimental import pallas as pl
from jax.experimental.pallas import tpu as pltpu
from jax.sharding import Mesh, PartitionSpec as P

D = 2880
QUERY_HEADS = 64
KEY_VALUE_HEADS = 8
HEAD_SIZE = 64
VISIBLE_TOKENS = 128
TOPK = 4

SEQ = ("y", "z")
ROW_CONTRACT = (((0,), (0,)), ((), ()))


def from_previous_block(keys, values):
    count = lax.axis_size("y") * lax.axis_size("z")
    both = jnp.concatenate([keys, values], axis=1)
    both = lax.ppermute(both, SEQ, [(source, source + 1) for source in range(count - 1)])
    return both[:, : keys.shape[1]], both[:, keys.shape[1] :]


def swap_y_and_f(value):
    side, depth = lax.axis_size("y"), lax.axis_size("z")
    pairs = [
        ((y * depth + z) * side + f, (f * depth + z) * side + y)
        for y in range(side)
        for z in range(depth)
        for f in range(side)
    ]
    return lax.ppermute(value, ("y", "z", "f"), pairs)


def to_all(value, axis):
    copies = jnp.broadcast_to(value[None], (lax.axis_size(axis), *value.shape))
    return lax.all_to_all(copies, axis, split_axis=0, concat_axis=0, tiled=True)


def double_stack(stack, axis):
    step = stack.shape[0]
    count = lax.axis_size(axis)
    other = lax.ppermute(stack, axis, [(i, i ^ step) for i in range(count)])
    return ordered(stack, other, (lax.axis_index(axis) & step) != 0)


def ordered(mine, other, second, axis=0):
    return jnp.where(
        second,
        jnp.concatenate([other, mine], axis=axis),
        jnp.concatenate([mine, other], axis=axis),
    )


P_PARTNER = [3, 2, 1, 0]
Q_PARTNER = [1, 0, 3, 2]
P_OF = [0, 0, 1, 1]
Q_OF = [0, 1, 1, 0]


def from_core(value):
    return lax.ppermute(value, "f", [(f, f ^ 1) for f in range(8)])


def from_chip(value, partner):
    return lax.ppermute(value, "f", [(f, 2 * partner[f // 2] + f % 2) for f in range(8)])


def of_chip_pair(value):
    groups = [[f, 2 * P_PARTNER[f // 2] + f % 2] for f in range(8) if P_OF[f // 2] == 0]
    return lax.all_gather(value, "f", axis=0, axis_index_groups=groups, tiled=True)


def hidden_kernel(own_ref, other_ref, *refs):
    *weight_refs, out_ref = refs
    aligned = D // 128 * 128
    rows = jnp.concatenate([own_ref[...], other_ref[...]], axis=0)
    scale = jnp.sum(
        rows[:, aligned : aligned + 128].astype(jnp.float32).T[D - aligned : D - aligned + 3],
        axis=0,
        keepdims=True,
    )
    weights = jnp.concatenate([ref[...] for ref in weight_refs], axis=0)
    products = scale * lax.dot_general(
        weights, rows, (((1,), (1,)), ((), ())), preferred_element_type=jnp.float32
    )
    units = weight_refs[0].shape[0] // 2
    for part in range(out_ref.shape[0]):
        gate_val = products[2 * part * units : (2 * part + 1) * units]
        up_val = products[(2 * part + 1) * units : (2 * part + 2) * units]
        hidden = gate_val * jax.nn.sigmoid(1.702 * gate_val) * (up_val + 1.0)
        out_ref[part, 0] = hidden.astype(jnp.bfloat16)


def hidden_of(own_rows, other_rows, weights):
    parts, units = len(weights), weights[0].shape[0] // 4
    count, width = own_rows.shape
    whole = pl.BlockSpec((count, width), lambda p: (0, 0))
    return pl.pallas_call(
        hidden_kernel,
        grid=(2,),
        out_shape=jax.ShapeDtypeStruct((parts, 2, units, 2 * count), jnp.bfloat16),
        in_specs=[whole, whole] + [pl.BlockSpec((2 * units, width), lambda p: (p, 0))] * len(weights),
        out_specs=pl.BlockSpec((parts, 1, units, 2 * count), lambda p: (0, p, 0, 0)),
        compiler_params=pltpu.CompilerParams(vmem_limit_bytes=24 << 20),
        cost_estimate=pl.CostEstimate(
            flops=16 * count * width * parts * units,
            bytes_accessed=4 * (count * width + 2 * parts * units * width),
            transcendentals=4 * parts * units * count,
        ),
    )(own_rows, other_rows, *weights)


def attend(queries, key_vectors, head_value_vectors, head_sink_logits, previous):
    tok_rows = queries.shape[0]
    key_heads = key_vectors.shape[1] // HEAD_SIZE
    query_grouping = QUERY_HEADS // KEY_VALUE_HEADS
    prev_keys, prev_values = previous
    all_keys = jnp.concatenate([prev_keys, key_vectors], axis=0).reshape(
        2 * tok_rows, key_heads, HEAD_SIZE
    )
    all_values = jnp.concatenate([prev_values, head_value_vectors], axis=0).reshape(
        2 * tok_rows, key_heads, HEAD_SIZE
    )
    query_heads = queries.reshape(tok_rows, key_heads, query_grouping, HEAD_SIZE)
    scores = jnp.einsum(
        "tkgd,skd->kgts", query_heads, all_keys, preferred_element_type=jnp.float32
    ) * HEAD_SIZE ** (-0.5)
    offset = lax.axis_index(SEQ) * tok_rows
    query_pos = offset + jnp.arange(tok_rows, dtype=jnp.int32)
    key_pos = offset - tok_rows + jnp.arange(2 * tok_rows, dtype=jnp.int32)
    valid = (
        (key_pos[None, :] >= 0)
        & (key_pos[None, :] <= query_pos[:, None])
        & (key_pos[None, :] > query_pos[:, None] - VISIBLE_TOKENS)
    )
    scores = jnp.where(valid, scores, -1e30)
    sink_entries = head_sink_logits.reshape(key_heads, query_grouping)[:, :, None]
    highest = jnp.maximum(jnp.max(scores, axis=-1), sink_entries)
    powers = jnp.exp(scores - highest[..., None])
    denom = jnp.sum(powers, axis=-1) + jnp.exp(sink_entries - highest)
    weights = (powers / denom[..., None]).astype(jnp.bfloat16)
    attended = jnp.einsum("kgts,skd->tkgd", weights, all_values, preferred_element_type=jnp.float32)
    return attended.astype(jnp.bfloat16).reshape(tok_rows, key_heads * query_grouping * HEAD_SIZE)


def places_of(ids, experts, capacity):
    tok_rows = ids.shape[0]
    onehot = (ids[:, :, None] == jnp.arange(experts, dtype=jnp.int32)).astype(jnp.float32)
    counts = jnp.sum(onehot, axis=1)
    row_index = jnp.arange(tok_rows, dtype=jnp.int32)
    strictly_lower = (row_index[:, None] > row_index[None, :]).astype(jnp.bfloat16)
    before = jnp.dot(
        strictly_lower, counts.astype(jnp.bfloat16), preferred_element_type=jnp.float32
    )
    slot = jnp.sum(onehot * before[:, None, :], axis=-1)
    return ids * capacity + slot.astype(jnp.int32)


def three_terms(value):
    terms = []
    for _ in range(3):
        term = value.astype(jnp.bfloat16).astype(jnp.float32)
        terms.append(term)
        value = value - term
    return terms


def to_slots(dest, rows, slots_ref):
    step = 256
    for start in range(0, slots_ref.shape[0], step):
        row = start + lax.broadcasted_iota(jnp.int32, (step, dest.shape[1]), 0)
        placing = (row == dest[0:1]).astype(jnp.float32)
        for j in range(1, TOPK):
            placing = placing + (row == dest[j : j + 1]).astype(jnp.float32)
        slots_ref[start : start + step, :] = jnp.dot(
            placing.astype(jnp.bfloat16), rows, preferred_element_type=jnp.float32
        ).astype(jnp.bfloat16)


def slots_kernel(dest_ref, rows_ref, slots_ref):
    to_slots(dest_ref[...], rows_ref[...], slots_ref)


def pack_kernel(
    spare, experts, parts_ref, packed_ref, features_ref, dest_ref, updated_ref, slots_ref
):
    aligned = spare // 128 * 128
    residual = packed_ref[...].astype(jnp.float32)
    column = lax.broadcasted_iota(jnp.int32, residual.shape, 1)
    updated = jnp.where(column < spare, residual, 0.0)
    for part in range(parts_ref.shape[0]):
        updated = updated + parts_ref[part].astype(jnp.float32)
    updated_ref[...] = updated
    gain = jnp.sum(features_ref[experts:].astype(jnp.float32), axis=0, keepdims=True)
    gained = updated * gain
    logits = lax.dot_general(
        gained,
        features_ref[:experts].astype(jnp.float32),
        (((1,), (1,)), ((), ())),
        precision=lax.Precision.HIGHEST,
        preferred_element_type=jnp.float32,
    )
    expert = lax.broadcasted_iota(jnp.int32, logits.shape, 1).astype(jnp.float32)
    last = gained[:, aligned:]
    lane = lax.broadcasted_iota(jnp.int32, last.shape, 1) - (spare - aligned)
    sums = [jnp.sum(updated * updated, axis=1, keepdims=True)]
    ids = []
    for j in range(TOPK):
        ids.append(
            jnp.sum(jnp.where(lane == j, residual[:, aligned:], 0.0), axis=1, keepdims=True)
        )
        sums.append(jnp.sum(jnp.where(expert == ids[j], logits, 0.0), axis=1, keepdims=True))
    terms = [three_terms(value) for value in sums]
    extras = [terms[i][k] for k in range(3) for i in range(1 + TOPK)]
    extras += [number + 1.0 for number in ids]
    for i, value in enumerate(extras):
        last = jnp.where(lane == i, value, last)
    rows = jnp.concatenate([gained[:, :aligned], last], axis=1).astype(jnp.bfloat16)
    to_slots(dest_ref[...], rows, slots_ref)


def unpack_kernel(spare, expert_ref, arrived_ref, rows_ref, side_ref):
    aligned = spare // 128 * 128
    first = arrived_ref[0][:, aligned:].astype(jnp.float32)
    total = first
    for chunk in range(arrived_ref.shape[0]):
        part = arrived_ref[chunk]
        if chunk:
            total = total + part[:, aligned:].astype(jnp.float32)
        rows_ref[:, chunk * spare : (chunk + 1) * spare] = part[:, :spare]
    lane = lax.broadcasted_iota(jnp.int32, total.shape, 1) - (spare - aligned)
    sums = []
    for i in range(1 + TOPK):
        wanted = (lane == i) | (lane == i + 1 + TOPK) | (lane == i + 2 * (1 + TOPK))
        sums.append(jnp.sum(jnp.where(wanted, total, 0.0), axis=1, keepdims=True))
    scale = lax.rsqrt(sums[0] / D + 1e-05)
    chosen = [value * scale for value in sums[1:]]
    highest = chosen[0]
    for value in chosen[1:]:
        highest = jnp.maximum(highest, value)
    powers = [jnp.exp(value - highest) for value in chosen]
    denom = sum(powers)
    own = (expert_ref[0] + 1).astype(jnp.float32)
    gate = jnp.zeros_like(scale)
    for j in range(TOPK):
        number = jnp.sum(
            jnp.where(lane == 3 * (1 + TOPK) + j, first, 0.0), axis=1, keepdims=True
        )
        gate = gate + jnp.where(number == own, powers[j] / denom, 0.0)
    column = lax.broadcasted_iota(jnp.int32, total.shape, 1)
    side_ref[...] = jnp.where(column == 0, gate, 0.0).T[: side_ref.shape[0]]
    column = column[:, : rows_ref.shape[1] - D]
    spare_columns = jnp.zeros(column.shape, jnp.float32)
    for i, term in enumerate(three_terms(scale)):
        spare_columns = jnp.where(column == i, term, spare_columns)
    rows_ref[:, D:] = spare_columns.astype(jnp.bfloat16)


def down_kernel(device_at, chips_with, units, hidden_ref, weight_ref, out_ref):
    height = hidden_ref.shape[0] // len(device_at)
    rows = out_ref.shape[1]
    for p in range(2):
        for c in range(2):
            total = None
            for q in range(2):
                start = device_at[p, q, c] * height
                for half, x in enumerate(chips_with[q]):
                    term = lax.dot_general(
                        hidden_ref[start + half * units : start + (half + 1) * units, :],
                        weight_ref[x * units : (x + 1) * units, :],
                        ROW_CONTRACT,
                        preferred_element_type=jnp.float32,
                    )
                    total = term if total is None else total + term
            for q in range(2):
                f = device_at[p, q, c]
                gate = gate_column(hidden_ref, f * height + 2 * units, rows)
                out_ref[f] = (total[q * rows : (q + 1) * rows] * gate).astype(jnp.bfloat16)


def gate_column(hidden_ref, start, rows):
    gate = hidden_ref[start : start + 16, :rows].astype(jnp.float32)[:1]
    return jnp.broadcast_to(gate, (rows, rows)).T[:, :1]


def grad_kernel(device_at, chips_with, units, hidden_ref, cotangent_ref, out_ref, grad_ref):
    height = hidden_ref.shape[0] // len(device_at)
    rows = cotangent_ref.shape[0] // len(device_at)
    kept, chunk = out_ref.shape[1:]
    order = [device_at[p, r, c] for p in range(2) for c in range(2) for r in range(2)]
    for i, f in enumerate(order):
        gate = gate_column(hidden_ref, f * height + 2 * units, rows)
        block = cotangent_ref[f * rows : (f + 1) * rows, :].astype(jnp.float32) * gate
        grad_ref[i * rows : (i + 1) * rows, :] = block.astype(jnp.bfloat16)
    for q in range(2):
        for half, x in enumerate(chips_with[q]):
            total = None
            for p in range(2):
                for c in range(2):
                    start = device_at[p, q, c] * height + half * units
                    first = 2 * (2 * p + c) * rows
                    term = jnp.dot(
                        hidden_ref[start : start + units, :],
                        grad_ref[first : first + 2 * rows, :],
                        preferred_element_type=jnp.float32,
                    )
                    total = term if total is None else total + term
            for c in range(2):
                part = total[c * units // 2 : c * units // 2 + kept, :chunk]
                out_ref[2 * x + c] = part.astype(jnp.bfloat16)


IN_VMEM = pl.BlockSpec(memory_space=pltpu.VMEM)


def local_call(kernel, outs, operands, scalars=(), flops=0, transcendentals=0):
    moved = sum(x.size * x.dtype.itemsize for x in (*operands, *outs))
    return pl.pallas_call(
        kernel,
        out_shape=outs,
        in_specs=[pl.BlockSpec(memory_space=pltpu.SMEM)] * len(scalars) + [IN_VMEM] * len(operands),
        out_specs=[IN_VMEM] * len(outs),
        compiler_params=pltpu.CompilerParams(vmem_limit_bytes=16 << 20),
        cost_estimate=pl.CostEstimate(
            flops=flops, bytes_accessed=moved, transcendentals=transcendentals
        ),
    )(*scalars, *operands)


def body(
    queries,
    key_vectors,
    head_value_vectors,
    head_sink_logits,
    out_weight,
    residual,
    norm_gain,
    router_weight,
    expert_ids,
    gate_weight,
    up_weight,
    down_weight,
    cotangent,
):
    tok_rows, chunk = residual.shape
    side, depth = lax.axis_size("y"), lax.axis_size("z")
    experts = router_weight.shape[1]
    capacity = 2 * TOPK * tok_rows // experts
    hidden_part = gate_weight.shape[2]

    place = lax.axis_index("f")
    core, chip = place & 1, place >> 1
    in_second_q = (chip == 1) | (chip == 2)
    units = -(-hidden_part // 16) * 16
    more_units = ((0, units - hidden_part), (0, 0))
    more_lanes = (more_units[0], (0, -D % 128))
    own_weights = jnp.concatenate(
        [jnp.pad(gate_weight[0].T, more_lanes), jnp.pad(up_weight[0].T, more_lanes)], axis=0
    )
    wide = -(-chunk // 128) * 128

    packed = jnp.concatenate([residual, expert_ids.astype(jnp.bfloat16)], axis=1)
    packed = swap_y_and_f(jnp.pad(packed, ((0, 0), (0, wide - chunk - TOPK))))
    gain_rest, gain_terms = norm_gain, []
    for _ in range(3):
        term = lax.reduce_precision(gain_rest, exponent_bits=8, mantissa_bits=7)
        gain_rest = gain_rest - term
        gain_terms.append(term.astype(jnp.bfloat16))
    features = jnp.concatenate([router_weight.T, jnp.stack(gain_terms)], axis=0)
    features = swap_y_and_f(jnp.pad(features, ((0, 13), (0, wide - chunk))))

    previous = from_previous_block(key_vectors, head_value_vectors)
    out_columns = double_stack(out_weight.T[None], "z")
    previous, out_columns = lax.optimization_barrier((previous, out_columns))
    attended = attend(queries, key_vectors, head_value_vectors, head_sink_logits, previous)
    attended, packed, own_weights = lax.optimization_barrier((attended, packed, own_weights))
    pair_weights = of_chip_pair(own_weights)
    attended_all = to_all(attended, "y").reshape(side * tok_rows, attended.shape[1])
    while out_columns.shape[0] < depth:
        out_columns = double_stack(out_columns, "z")
    out_columns = out_columns.reshape(chunk, out_weight.shape[0])
    out_columns = jnp.pad(out_columns, ((0, wide - chunk), (0, 0)))
    attended_all, features = lax.optimization_barrier((attended_all, features))

    partial_out = lax.dot_general(
        attended_all, out_columns, (((1,), (1,)), ((), ())), preferred_element_type=jnp.float32
    )
    partial_out = partial_out.astype(jnp.bfloat16).reshape(side, tok_rows, wide)
    parts = lax.all_to_all(partial_out, "f", split_axis=0, concat_axis=0, tiled=True)
    ids_here = packed[:tok_rows, chunk : chunk + TOPK].astype(jnp.int32)
    dest_here = places_of(ids_here, experts, capacity).T
    updated_here, local_slots = local_call(
        functools.partial(pack_kernel, chunk, experts),
        [
            jax.ShapeDtypeStruct((tok_rows, wide), jnp.float32),
            jax.ShapeDtypeStruct((experts * capacity, wide), jnp.bfloat16),
        ],
        (parts, packed, features, dest_here),
        flops=2 * experts * capacity * tok_rows * wide,
    )
    local_slots = local_slots.reshape(experts, capacity, wide)
    arrived = lax.all_to_all(local_slots, SEQ, split_axis=0, concat_axis=0, tiled=True)

    updated = swap_y_and_f(updated_here)[:, :chunk]
    dest = places_of(expert_ids, experts, capacity)
    slot_row = jnp.arange(experts * capacity, dtype=jnp.int32)
    placing = jnp.any(dest[:, :, None] == slot_row, axis=1).astype(jnp.bfloat16)

    expert_rows, sums = local_call(
        functools.partial(unpack_kernel, chunk),
        [
            jax.ShapeDtypeStruct((depth * capacity, -(-D // 128) * 128), jnp.bfloat16),
            jax.ShapeDtypeStruct((8, depth * capacity), jnp.float32),
        ],
        (arrived.reshape(side, depth * capacity, wide),),
        scalars=(lax.axis_index(SEQ).astype(jnp.int32)[None],),
    )
    own_gate = sums[:1].astype(jnp.bfloat16)
    other_rows = from_chip(expert_rows, Q_PARTNER)
    expert_rows, pair_weights = lax.optimization_barrier((expert_rows, pair_weights))
    core_weights = from_core(pair_weights)
    cotangent_slots = local_call(
        slots_kernel,
        [jax.ShapeDtypeStruct((experts * capacity, wide), jnp.bfloat16)],
        (dest.T, jnp.pad(cotangent, ((0, 0), (0, wide - chunk)))),
        flops=2 * experts * capacity * tok_rows * wide,
    )[0].reshape(experts, capacity, wide)
    other_rows, updated = lax.optimization_barrier((other_rows, updated))
    hidden_units = hidden_of(expert_rows, other_rows, [pair_weights, core_weights])
    hidden_units, cotangent_slots = lax.optimization_barrier((hidden_units, cotangent_slots))
    cotangent_arrived = lax.all_to_all(cotangent_slots, SEQ, split_axis=0, concat_axis=0, tiled=True)
    rows_per_device = depth * capacity
    hidden_units = ordered(hidden_units[0], hidden_units[1], core == 1, axis=1)
    hidden_units = hidden_units.reshape(4 * units, 2 * rows_per_device)
    hidden_units = jnp.where(
        in_second_q,
        jnp.concatenate(
            [hidden_units[:, rows_per_device:], hidden_units[:, :rows_per_device]], axis=1
        ),
        hidden_units,
    )
    gate_row = jnp.pad(own_gate, ((0, 15), (0, depth * capacity)))
    hidden_units = jnp.concatenate([hidden_units, gate_row], axis=0)
    gathered = lax.all_gather(hidden_units, "f", axis=0, tiled=True)

    device_at = {(P_OF[f // 2], Q_OF[f // 2], f % 2): f for f in range(8)}
    chips_with = [[x for x in range(4) if Q_OF[x] == q] for q in range(2)]
    down_rows = down_weight[0].reshape(side, hidden_part, chunk)
    down_rows = jnp.pad(down_rows, ((0, 0), *more_units)).reshape(side * units, chunk)
    expert_output = local_call(
        functools.partial(down_kernel, device_at, chips_with, 2 * units),
        [jax.ShapeDtypeStruct((side, depth * capacity, chunk), jnp.bfloat16)],
        (gathered, down_rows),
        flops=2 * experts * capacity * down_weight.shape[1] * chunk,
    )[0].reshape(experts, capacity, chunk)
    cotangent_arrived, expert_output = lax.optimization_barrier((cotangent_arrived, expert_output))
    returned = lax.all_to_all(expert_output, SEQ, split_axis=0, concat_axis=0, tiled=True)
    returned = returned.reshape(experts * capacity, chunk)
    mixture = jnp.dot(placing, returned, preferred_element_type=jnp.float32)
    layer_output = (updated + mixture).astype(jnp.bfloat16)
    grad_local = pl.pallas_call(
        functools.partial(grad_kernel, device_at, chips_with, 2 * units),
        out_shape=jax.ShapeDtypeStruct((side, hidden_part, chunk), jnp.bfloat16),
        in_specs=[IN_VMEM] * 2,
        out_specs=IN_VMEM,
        scratch_shapes=[pltpu.VMEM((experts * capacity, wide), jnp.bfloat16)],
        compiler_params=pltpu.CompilerParams(vmem_limit_bytes=16 << 20),
        cost_estimate=pl.CostEstimate(
            flops=2 * experts * capacity * side * units * wide,
            bytes_accessed=2 * (gathered.size + 2 * experts * capacity * wide),
            transcendentals=0,
        ),
    )(gathered, cotangent_arrived.reshape(experts * capacity, wide))
    return (layer_output, grad_local.reshape(1, side * hidden_part, chunk))


def solution(mesh):
    seq, ffn = mesh.devices.shape
    side = math.isqrt(seq)
    grid = Mesh(mesh.devices.reshape(side, seq // side, ffn), ("y", "z", "f"))
    return jax.shard_map(
        body,
        mesh=grid,
        in_specs=(
            P(SEQ, "f"),
            P(SEQ, "f"),
            P(SEQ, "f"),
            P("f"),
            P("f", SEQ),
            P(SEQ, "f"),
            P("f"),
            P("f", None),
            P(SEQ, None),
            P(SEQ, None, "f"),
            P(SEQ, None, "f"),
            P(SEQ, None, "f"),
            P(SEQ, "f"),
        ),
        out_specs=(P(SEQ, "f"), P(SEQ, None, "f")),
        check_vma=False,
    )
```

time: 262 us -> 251 us (0.958)
  matrix products: 23.1 us -> 3.96 us
  starting transfers between devices: 58.7 us -> 73.6 us
  Pallas kernels: 0 us -> 12.7 us
  blocking collectives: 44.7 us -> 32.7 us
  waiting for transfers between devices: 101 us -> 89.3 us
    all_to_all x1, waiting for transfers between devices: 21 us -> 0.01 us  [body(): lax.all_to_all(cotangent_slots, SEQ, split_axis=0, concat_axis=0, tiled=T...]
    dot_general x11 -> x3, matrix products: 21.9 us -> 1.69 us  [the longest x1 1.42 us: body(): mixture = jnp.dot(placing, returned, preferred_element_type=jnp.float32)]
    all_gather x2, waiting for transfers between devices: 0.04 us -> 19.5 us  [the longest x1 19.5 us: body(): gathered = lax.all_gather(hidden_units, 'f', axis=0, tiled=True)]
    ppermute x2 -> x6, starting transfers between devices: 8.68 us -> 27.1 us  [the longest x3 19.8 us: double_stack(): other = lax.ppermute(stack, axis, [(i, i ^ step) for i in range(count)])]
    ppermute x2 -> x6, waiting for transfers between devices: 0.01 us -> 16.6 us  [the longest x1 10.7 us: from_chip(): lax.ppermute(value, 'f', [(f, 2 * partner[f // 2] + f % 2) for f in range...]
    all_gather x1 -> x0, blocking collectives: 14 us -> none  [body(): lax.all_gather(jnp.concatenate([logits_part, square_part], axis=1).T, 'f'...]
    all_to_all x2 -> x1, waiting for transfers between devices: 13.4 us -> 0.01 us  [to_all(): return lax.all_to_all(copies, axis, split_axis=0, concat_axis=0, tiled=True)]
    pallas_call x0 -> x6, Pallas kernels: none -> 12.7 us  [the longest x4 4.82 us: local_call(): pl.pallas_call(kernel, out_shape=outs, in_specs=[pl.BlockSpec(memory_spac...]
  transfers between devices with their start and end apart: 13 -> 15, of which waited for: 7 -> 9; matrix products, arithmetic and copies ran while one was open for 9% -> 6% of each run, Pallas kernels for 0% -> 3%
where the time goes in v2:
time: 251 us; the launch traced here: 250 us
  waiting for transfers between devices  89.3 us (36%)
  starting transfers between devices  73.6 us (29%)
  blocking collectives  32.7 us (13%)
  between operations  14.6 us (6%)
  local copies, waits for them, and re-layouts  13.6 us (5%)
  Pallas kernels  12.7 us (5%)
  other arithmetic  9.18 us (4%)
  matrix products  3.96 us (2%)
    all_to_all x1, blocking collectives, body(): lax.all_to_all(local_slots, SEQ, split_axis=0, concat_axis=0, tiled=True)  32.7 us
    ppermute x3, starting transfers between devices, double_stack(): other = lax.ppermute(stack, axis, [(i, i ^ step) for i in range(count)])  19.8 us
    all_gather x1, waiting for transfers between devices, body(): gathered = lax.all_gather(hidden_units, 'f', axis=0, tiled=True)  19.5 us
    all_to_all x1, waiting for transfers between devices, body(): lax.all_to_all(expert_output, SEQ, split_axis=0, concat_axis=0, tiled=True)  18.3 us
    ppermute x3, waiting for transfers between devices, swap_y_and_f(): return lax.ppermute(value, ('y', 'z', 'f'), pairs)  17.3 us
    all_to_all x1, waiting for transfers between devices, body(): lax.all_to_all(partial_out, 'f', split_axis=0, concat_axis=0, tiled=True)  16.9 us
    all_to_all x1, starting transfers between devices, body(): lax.all_to_all(expert_output, SEQ, split_axis=0, concat_axis=0, tiled=True)  13.5 us
    all_to_all x1, starting transfers between devices, to_all(): return lax.all_to_all(copies, axis, split_axis=0, concat_axis=0, tiled=True)  11.6 us
  transfers between devices with their start and end apart: 15, of which 9 were waited for; matrix products, arithmetic and copies ran while one was open for 6% of the time, Pallas kernels for 3%

profile of v2, /device:TPU:16, one launch (start us, length us, event | category | flops | bytes accessed | tf_op | source)
XLA Modules:
  0.0 249.6 jit_solution(2629403114034751932)
XLA Ops:
  7.2 4.3 %collective-permute-start.1 = (bf16[1,45,512]{2,1,0:T(8,128)(2,1)}, bf16[1,45,512]{2,1,0:T(8,128)(2,1)S(1)}, u32[]{:S(2)}, u32[]{:S(2)}) collective-permute-start(bf16[1,45,512]{2,1,0:T(8,128)(2,1)} %bitcast.72), channel_id=1, source_target_pairs={{0,8},{8,0},{16,24},{24,16},{32,40},{40,32},{48,56},{56,48},{1,9},... | collective-permute-start | bytes 138248 | tf_op jit(solution)/shard_map/ppermute | solution.py:48
  12.2 1.9 collective-permute-start
  17.4 3.3 %collective-permute-start.2 = (bf16[128,384]{0,1:T(8,128)(2,1)S(1)}, bf16[128,384]{0,1:T(8,128)(2,1)S(1)}, u32[]{:S(2)}, u32[]{:S(2)}) collective-permute-start(bf16[128,384]{0,1:T(8,128)(2,1)S(1)} %fusion.18), channel_id=1, source_target_pairs={{0,0},{1,64},{2,128},{3,192},{4,256},{5,320},{6,384},{7,448},{8,8}... | collective-permute-start | bytes 294920 | tf_op jit(solution)/shard_map/ppermute | solution.py:37
  20.7 3.1 %fusion.2 = bf16[384,2944]{1,0:T(8,128)(2,1)} fusion(bf16[180,2880]{1,0:T(8,128)(2,1)} %bitcast.65, bf16[180,2880]{1,0:T(8,128)(2,1)} %bitcast.66), kind=kLoop, calls=%fused_computation.4 | loop fusion | flops 9043968 | bytes 4334592 | tf_op jit(solution)/shard_map/concatenate | solution.py:363
  25.2 1.4 collective-permute-done.2
  27.8 11.6 %all-to-all-start = ((bf16[8,128,512]{2,1,0:T(8,128)(2,1)}), bf16[8,128,512]{2,1,0:T(8,128)(2,1)S(1)}, u32[]{:S(2)}, u32[]{:S(2)}) async-start(bf16[8,128,512]{2,1,0:T(8,128)(2,1)} %broadcast_in_dim.18), calls=%async_computation | async-start | bytes 2097152 | tf_op jit(solution)/shard_map/all_to_all | solution.py:42
  40.1 6.1 %collective-permute-start.4 = (bf16[2,45,512]{2,1,0:T(8,128)(2,1)S(1)}, bf16[2,45,512]{2,1,0:T(8,128)(2,1)S(1)}, u32[]{:S(2)}, u32[]{:S(2)}) collective-permute-start(bf16[2,45,512]{2,1,0:T(8,128)(2,1)S(1)} %maximum_select_fusion.4), channel_id=1, source_target_pairs={{0,16},{8,24},{16,0},{24,8},{32,48},{40,56},{48,32},{56,40},{1,17}... | collective-permute-start | bytes 276488 | tf_op jit(solution)/shard_map/ppermute | solution.py:48
  46.2 2.6 %collective-permute-done.4 = bf16[2,45,512]{2,1,0:T(8,128)(2,1)S(1)} collective-permute-done((bf16[2,45,512]{2,1,0:T(8,128)(2,1)S(1)}, bf16[2,45,512]{2,1,0:T(8,128)(2,1)S(1)}, u32[]{:S(2)}, u32[]{:S(2)}) %collective-permute-start.4) | collective-permute-done | bytes 92192 | tf_op jit(solution)/shard_map/ppermute | solution.py:48
  48.8 9.4 %collective-permute-start.5 = (bf16[4,45,512]{2,1,0:T(8,128)(2,1)S(1)}, bf16[4,45,512]{2,1,0:T(8,128)(2,1)S(1)}, u32[]{:S(2)}, u32[]{:S(2)}) collective-permute-start(bf16[4,45,512]{2,1,0:T(8,128)(2,1)S(1)} %maximum_select_fusion.3), channel_id=1, source_target_pairs={{0,32},{8,40},{16,48},{24,56},{32,0},{40,8},{48,16},{56,24},{1,33}... | collective-permute-start | bytes 552968 | tf_op jit(solution)/shard_map/ppermute | solution.py:48
  58.3 1.9 collective-permute-start.3
  60.2 3.3 %collective-permute-done.5 = bf16[4,45,512]{2,1,0:T(8,128)(2,1)S(1)} collective-permute-done((bf16[4,45,512]{2,1,0:T(8,128)(2,1)S(1)}, bf16[4,45,512]{2,1,0:T(8,128)(2,1)S(1)}, u32[]{:S(2)}, u32[]{:S(2)}) %collective-permute-start.5) | collective-permute-done | bytes 184352 | tf_op jit(solution)/shard_map/ppermute | solution.py:48
  63.7 3.9 %collective-permute-done.3.features_ref = bf16[80,384]{1,0:T(8,128)(2,1)S(1)} collective-permute-done((bf16[80,384]{1,0:T(8,128)(2,1)S(1)}, bf16[80,384]{1,0:T(8,128)(2,1)S(1)}, u32[]{:S(2)}, u32[]{:S(2)}) %collective-permute-start.3) | collective-permute-done | bytes 61472 | tf_op jit(solution)/shard_map/ppermute | solution.py:37
  67.7 1.6 convolution_convert_fusion
  69.3 6.2 %all-to-all-start.1 = ((bf16[8,128,384]{2,1,0:T(8,128)(2,1)}), bf16[8,128,384]{2,1,0:T(8,128)(2,1)S(1)}, u32[]{:S(2)}, u32[]{:S(2)}) async-start(bf16[8,128,384]{2,1,0:T(8,128)(2,1)} %bitcast.19), calls=%async_computation.1 | async-start | bytes 1572864 | tf_op jit(solution)/shard_map/all_to_all | solution.py:395
  75.8 16.9 %all-to-all-done.1.parts_ref = bf16[8,128,384]{2,1,0:T(8,128)(2,1)S(1)} async-done(((bf16[8,128,384]{2,1,0:T(8,128)(2,1)}), bf16[8,128,384]{2,1,0:T(8,128)(2,1)S(1)}, u32[]{:S(2)}, u32[]{:S(2)}) %all-to-all-start.1) | async-done | bytes 786464 | tf_op jit(solution)/shard_map/all_to_all | solution.py:395
  93.7 32.7 %all_to_all.25 = bf16[64,16,384]{2,1,0:T(8,128)(2,1)S(1)} all-to-all(bf16[64,16,384]{2,1,0:T(8,128)(2,1)S(1)} %bitcast.62), channel_id=1, replica_groups=mesh['y'=8,'z'=8,'f'=8] {'y','z'}, dimensions={0} | all-to-all | bytes 1572864 | tf_op jit(solution)/shard_map/all_to_all | solution.py:408
  126.9 1.9 collective-permute-start.8
  128.8 3.5 %collective-permute-start.6 = (bf16[128,2944]{1,0:T(8,128)(2,1)S(1)}, bf16[128,2944]{1,0:T(8,128)(2,1)S(1)}, u32[]{:S(2)}, u32[]{:S(2)}) collective-permute-start(bf16[128,2944]{1,0:T(8,128)(2,1)S(1)} %get-tuple-element.34.own_ref), channel_id=1, source_target_pairs={{0,2},{1,3},{2,0},{3,1},{4,6},{5,7},{6,4},{7,5},{8,10},{9,11},{10,... | collective-permute-start | bytes 2261000 | tf_op jit(solution)/shard_map/ppermute | solution.py:71
  132.3 1.9 collective-permute-start.7
  135.7 12.0 %collective-permute-done.7 = f32[128,384]{1,0:T(8,128)S(1)} collective-permute-done((f32[128,384]{1,0:T(8,128)S(1)}, f32[128,384]{1,0:T(8,128)S(1)}, u32[]{:S(2)}, u32[]{:S(2)}) %collective-permute-start.7) | collective-permute-done | bytes 196640 | tf_op jit(solution)/shard_map/ppermute | solution.py:37
  147.7 10.7 %collective-permute-done.6.other_ref = bf16[128,2944]{1,0:T(8,128)(2,1)S(1)} collective-permute-done((bf16[128,2944]{1,0:T(8,128)(2,1)S(1)}, bf16[128,2944]{1,0:T(8,128)(2,1)S(1)}, u32[]{:S(2)}, u32[]{:S(2)}) %collective-permute-start.6) | collective-permute-done | bytes 753696 | tf_op jit(solution)/shard_map/ppermute | solution.py:71
  158.4 2.3 copy-done.4
  160.7 4.5 %shard_map.142 = bf16[2,2,192,256]{3,2,1,0:T(8,128)(2,1)S(1)} custom-call(bf16[128,2944]{1,0:T(8,128)(2,1)S(1)} %get-tuple-element.34.own_ref, bf16[128,2944]{1,0:T(8,128)(2,1)S(1)} %collective-permute-done.6.other_ref, bf16[768,2944]{1,0:T(8,128)(2,1)S(1)} %copy-done.4, bf16[768,2944]{1,0:T(8,128)(2,1)} %collective-permute-done.8.refs_1_), custom_call_target="tpu_custom_call" | custom-call | flops 2315255808 | bytes 10551296 | tf_op jit(solution)/shard_map/pallas_call | solution.py:104
  166.4 8.1 %all-to-all-start.3 = ((bf16[64,16,384]{2,1,0:T(8,128)(2,1)}), bf16[64,16,384]{2,1,0:T(8,128)(2,1)}, u32[]{:S(2)}, u32[]{:S(2)}) async-start(bf16[64,16,384]{2,1,0:T(8,128)(2,1)} %bitcast.24), calls=%async_computation.3 | async-start | bytes 1572864 | tf_op jit(solution)/shard_map/all_to_all | solution.py:437
  176.0 19.5 %all-gather.5.cloned.1.call-done.hidden_ref = bf16[6272,256]{1,0:T(8,128)(2,1)} async-done(((bf16[784,256]{1,0:T(8,128)(2,1)}), bf16[6272,256]{1,0:T(8,128)(2,1)}) %all-gather.5.cloned.1.call-update) | async-done | bytes 3211280 | tf_op jit(solution)/shard_map/all_gather | solution.py:450
  195.5 1.9 copy-done
  198.7 2.1 shard_map.144
  201.7 13.5 %all-to-all-start.4 = ((bf16[64,16,360]{2,1,0:T(8,128)(2,1)}), bf16[64,16,360]{2,1,0:T(8,128)(2,1)}, u32[]{:S(2)}, u32[]{:S(2)}) async-start(bf16[64,16,360]{2,1,0:T(8,128)(2,1)} %bitcast.60), calls=%async_computation.4 | async-start | bytes 1572864 | tf_op jit(solution)/shard_map/all_to_all | solution.py:463
  215.6 3.3 %shard_map.145 = bf16[8,180,360]{2,1,0:T(8,128)(2,1)S(1)} custom-call(bf16[6272,256]{1,0:T(8,128)(2,1)S(1)} %copy-done.1, bf16[1024,384]{1,0:T(8,128)(2,1)} %bitcast.31.cotangent_ref), custom_call_target="tpu_custom_call" | custom-call | flops 1207959552 | bytes 4784128 | tf_op jit(solution)/shard_map/pallas_call | solution.py:467
  220.0 2.3 reshape.165
  222.2 18.3 %all-to-all-done.4 = bf16[64,16,360]{2,1,0:T(8,128)(2,1)} async-done(((bf16[64,16,360]{2,1,0:T(8,128)(2,1)}), bf16[64,16,360]{2,1,0:T(8,128)(2,1)}, u32[]{:S(2)}, u32[]{:S(2)}) %all-to-all-start.4) | async-done | bytes 737312 | tf_op jit(solution)/shard_map/all_to_all | solution.py:463
  240.5 1.4 fusion.42
  (89 shorter events, 17.6 us)
Async XLA Ops:
  7.2 17.0 %collective-permute-start.1 = (bf16[1,45,512]{2,1,0:T(8,128)(2,1)}, bf16[1,45,512]{2,1,0:T(8,128)(2,1)S(1)}, u32[]{:S(2)}, u32[]{:S(2)}) collective-permute-start(bf16[1,45,512]{2,1,0:T(8,128)(2,1)} %bitcast.72), channel_id=1, source_target_pairs={{0,8},{8,0},{16,24},{24,16},{32,40},{40,32},{48,56},{56,48},{1,9},... | collective-permute-start | bytes 138248 | tf_op jit(solution)/shard_map/ppermute | solution.py:48
  12.2 12.0 %collective-permute-start = (bf16[128,128]{0,1:T(8,128)(2,1)S(1)}, bf16[128,128]{0,1:T(8,128)(2,1)S(1)}, u32[]{:S(2)}, u32[]{:S(2)}) collective-permute-start(bf16[128,128]{0,1:T(8,128)(2,1)S(1)} %pad_maximum_fusion), channel_id=1, source_target_pairs={{0,8},{8,16},{16,24},{24,32},{32,40},{40,48},{48,56},{56,64},{64,7... | collective-permute-start | bytes 98312 | tf_op jit(solution)/shard_map/ppermute | solution.py:25
  17.3 6.7 %copy-start.7 = (bf16[128,512]{1,0:T(8,128)(2,1)S(1)}, bf16[128,512]{1,0:T(8,128)(2,1)}, u32[]{:S(2)}) copy-start(bf16[128,512]{1,0:T(8,128)(2,1)} %param.13) | copy-start | bytes 393220
  17.4 9.2 %collective-permute-start.2 = (bf16[128,384]{0,1:T(8,128)(2,1)S(1)}, bf16[128,384]{0,1:T(8,128)(2,1)S(1)}, u32[]{:S(2)}, u32[]{:S(2)}) collective-permute-start(bf16[128,384]{0,1:T(8,128)(2,1)S(1)} %fusion.18), channel_id=1, source_target_pairs={{0,0},{1,64},{2,128},{3,192},{4,256},{5,320},{6,384},{7,448},{8,8}... | collective-permute-start | bytes 294920 | tf_op jit(solution)/shard_map/ppermute | solution.py:37
  20.7 3.5 %copy-start.11 = (bf16[512,45]{0,1:T(8,128)(2,1)S(1)}, bf16[512,45]{0,1:T(8,128)(2,1)}, u32[]{:S(2)}) copy-start(bf16[512,45]{0,1:T(8,128)(2,1)} %param.17) | copy-start | bytes 138244
  20.7 3.5 %copy-start.9 = (bf16[128,64]{0,1:T(8,128)(2,1)S(1)}, bf16[128,64]{0,1:T(8,128)(2,1)}, u32[]{:S(2)}) copy-start(bf16[128,64]{0,1:T(8,128)(2,1)} %param.14) | copy-start | bytes 49156
  20.7 3.9 %copy-start.13 = (f32[8]{0:T(128)S(1)}, f32[8]{0:T(128)}, u32[]{:S(2)}) copy-start(f32[8]{0:T(128)} %param.16) | copy-start | bytes 100
  23.9 1.0 copy-start.12
  27.8 30.4 %copy-start.14 = (f32[360]{0:T(512)S(1)}, f32[360]{0:T(512)}, u32[]{:S(2)}) copy-start(f32[360]{0:T(512)} %param.19) | copy-start | bytes 4324
  27.8 30.5 %copy-start.10 = (bf16[360,64]{0,1:T(8,128)(2,1)S(1)}, bf16[360,64]{0,1:T(8,128)(2,1)}, u32[]{:S(2)}) copy-start(bf16[360,64]{0,1:T(8,128)(2,1)} %param.20) | copy-start | bytes 138244
  27.8 39.9 %all-to-all-start = ((bf16[8,128,512]{2,1,0:T(8,128)(2,1)}), bf16[8,128,512]{2,1,0:T(8,128)(2,1)S(1)}, u32[]{:S(2)}, u32[]{:S(2)}) async-start(bf16[8,128,512]{2,1,0:T(8,128)(2,1)} %broadcast_in_dim.18), calls=%async_computation | async-start | bytes 2097152 | tf_op jit(solution)/shard_map/all_to_all | solution.py:42
  39.4 87.5 %all-gather.3.cloned.1.call-start = ((), (), s32[]{:S(2)}) async-start(), calls=%async_computation.5 | async-start | bytes 6782976 | tf_op jit(solution)/shard_map/all_gather | solution.py:76
  40.1 8.7 %collective-permute-start.4 = (bf16[2,45,512]{2,1,0:T(8,128)(2,1)S(1)}, bf16[2,45,512]{2,1,0:T(8,128)(2,1)S(1)}, u32[]{:S(2)}, u32[]{:S(2)}) collective-permute-start(bf16[2,45,512]{2,1,0:T(8,128)(2,1)S(1)} %maximum_select_fusion.4), channel_id=1, source_target_pairs={{0,16},{8,24},{16,0},{24,8},{32,48},{40,56},{48,32},{56,40},{1,17}... | collective-permute-start | bytes 276488 | tf_op jit(solution)/shard_map/ppermute | solution.py:48
  48.8 14.7 %collective-permute-start.5 = (bf16[4,45,512]{2,1,0:T(8,128)(2,1)S(1)}, bf16[4,45,512]{2,1,0:T(8,128)(2,1)S(1)}, u32[]{:S(2)}, u32[]{:S(2)}) collective-permute-start(bf16[4,45,512]{2,1,0:T(8,128)(2,1)S(1)} %maximum_select_fusion.3), channel_id=1, source_target_pairs={{0,32},{8,40},{16,48},{24,56},{32,0},{40,8},{48,16},{56,24},{1,33}... | collective-permute-start | bytes 552968 | tf_op jit(solution)/shard_map/ppermute | solution.py:48
  58.3 9.4 %collective-permute-start.3 = (bf16[80,384]{1,0:T(8,128)(2,1)S(1)}, bf16[80,384]{1,0:T(8,128)(2,1)S(1)}, u32[]{:S(2)}, u32[]{:S(2)}) collective-permute-start(bf16[80,384]{1,0:T(8,128)(2,1)S(1)} %fusion.24), channel_id=1, source_target_pairs={{0,0},{1,64},{2,128},{3,192},{4,256},{5,320},{6,384},{7,448},{8,8}... | collective-permute-start | bytes 184328 | tf_op jit(solution)/shard_map/ppermute | solution.py:37
  69.3 65.0 %copy-start.8 = (bf16[128,360]{0,1:T(8,128)(2,1)S(1)}, bf16[128,360]{0,1:T(8,128)(2,1)}, u32[]{:S(2)}) copy-start(bf16[128,360]{0,1:T(8,128)(2,1)} %param.25) | copy-start | bytes 276484
  69.3 23.5 %all-to-all-start.1 = ((bf16[8,128,384]{2,1,0:T(8,128)(2,1)}), bf16[8,128,384]{2,1,0:T(8,128)(2,1)S(1)}, u32[]{:S(2)}, u32[]{:S(2)}) async-start(bf16[8,128,384]{2,1,0:T(8,128)(2,1)} %bitcast.19), calls=%async_computation.1 | async-start | bytes 1572864 | tf_op jit(solution)/shard_map/all_to_all | solution.py:395
  75.4 120.1 %all-gather.5.cloned.1.call-start = ((), (), s32[]{:S(2)}) async-start(), calls=%async_computation.6 | async-start | bytes 3612672 | tf_op jit(solution)/shard_map/all_gather | solution.py:450
  126.9 31.5 %collective-permute-start.8 = (bf16[768,2944]{1,0:T(8,128)(2,1)}, bf16[768,2944]{1,0:T(8,128)(2,1)}, u32[]{:S(2)}, u32[]{:S(2)}) collective-permute-start(bf16[768,2944]{1,0:T(8,128)(2,1)} %all-gather.3.cloned.1.call-done.refs_0_), channel_id=1, source_target_pairs={{0,1},{1,0},{2,3},{3,2},{4,5},{5,4},{6,7},{7,6},{8,9},{9,8},{10,11... | collective-permute-start | bytes 13565960 | tf_op jit(solution)/shard_map/ppermute | solution.py:67
  128.8 29.6 %collective-permute-start.6 = (bf16[128,2944]{1,0:T(8,128)(2,1)S(1)}, bf16[128,2944]{1,0:T(8,128)(2,1)S(1)}, u32[]{:S(2)}, u32[]{:S(2)}) collective-permute-start(bf16[128,2944]{1,0:T(8,128)(2,1)S(1)} %get-tuple-element.34.own_ref), channel_id=1, source_target_pairs={{0,2},{1,3},{2,0},{3,1},{4,6},{5,7},{6,4},{7,5},{8,10},{9,11},{10,... | collective-permute-start | bytes 2261000 | tf_op jit(solution)/shard_map/ppermute | solution.py:71
  132.3 15.4 %collective-permute-start.7 = (f32[128,384]{1,0:T(8,128)S(1)}, f32[128,384]{1,0:T(8,128)S(1)}, u32[]{:S(2)}, u32[]{:S(2)}) collective-permute-start(f32[128,384]{1,0:T(8,128)S(1)} %get-tuple-element.31), channel_id=1, source_target_pairs={{0,0},{1,64},{2,128},{3,192},{4,256},{5,320},{6,384},{7,448},{8,8}... | collective-permute-start | bytes 589832 | tf_op jit(solution)/shard_map/ppermute | solution.py:37
  158.4 2.3 copy-start.4
  165.4 9.2 %copy-start.6 = (bf16[1,1440,360]{2,1,0:T(8,128)(2,1)S(1)}, bf16[1,1440,360]{2,1,0:T(8,128)(2,1)}, u32[]{:S(2)}) copy-start(bf16[1,1440,360]{2,1,0:T(8,128)(2,1)} %param.24) | copy-start | bytes 3110404
  166.4 35.3 %all-to-all-start.3 = ((bf16[64,16,384]{2,1,0:T(8,128)(2,1)}), bf16[64,16,384]{2,1,0:T(8,128)(2,1)}, u32[]{:S(2)}, u32[]{:S(2)}) async-start(bf16[64,16,384]{2,1,0:T(8,128)(2,1)} %bitcast.24), calls=%async_computation.3 | async-start | bytes 1572864 | tf_op jit(solution)/shard_map/all_to_all | solution.py:437
  195.5 1.9 copy-start
  197.4 1.3 copy-start.2
  198.7 16.9 %copy-start.1 = (bf16[6272,256]{1,0:T(8,128)(2,1)S(1)}, bf16[6272,256]{1,0:T(8,128)(2,1)}, u32[]{:S(2)}) copy-start(bf16[6272,256]{1,0:T(8,128)(2,1)} %all-gather.5.cloned.1.call-done.hidden_ref) | copy-start | bytes 9633796
  200.8 0.9 copy-start.5
  201.7 38.8 %all-to-all-start.4 = ((bf16[64,16,360]{2,1,0:T(8,128)(2,1)}), bf16[64,16,360]{2,1,0:T(8,128)(2,1)}, u32[]{:S(2)}, u32[]{:S(2)}) async-start(bf16[64,16,360]{2,1,0:T(8,128)(2,1)} %bitcast.60), calls=%async_computation.4 | async-start | bytes 1572864 | tf_op jit(solution)/shard_map/all_to_all | solution.py:463
  219.0 1.0 copy-start.3
Sparse Core Ops, SparseCore 0:
  42.3 81.3 all-gather.2
  166.5 28.9 all-gather.4

commit v3 on v2

--- a/solution.py
+++ b/solution.py
@@ -76,44 +76,42 @@
     return lax.all_gather(value, "f", axis=0, axis_index_groups=groups, tiled=True)
 
 
-def hidden_kernel(own_ref, other_ref, *refs):
-    *weight_refs, out_ref = refs
+def hidden_kernel(*refs):
+    *row_refs, weight_ref, out_ref = refs
     aligned = D // 128 * 128
-    rows = jnp.concatenate([own_ref[...], other_ref[...]], axis=0)
+    rows = jnp.concatenate([ref[...] for ref in row_refs], axis=0)
     scale = jnp.sum(
         rows[:, aligned : aligned + 128].astype(jnp.float32).T[D - aligned : D - aligned + 3],
         axis=0,
         keepdims=True,
     )
-    weights = jnp.concatenate([ref[...] for ref in weight_refs], axis=0)
     products = scale * lax.dot_general(
-        weights, rows, (((1,), (1,)), ((), ())), preferred_element_type=jnp.float32
-    )
-    units = weight_refs[0].shape[0] // 2
-    for part in range(out_ref.shape[0]):
-        gate_val = products[2 * part * units : (2 * part + 1) * units]
-        up_val = products[(2 * part + 1) * units : (2 * part + 2) * units]
-        hidden = gate_val * jax.nn.sigmoid(1.702 * gate_val) * (up_val + 1.0)
-        out_ref[part, 0] = hidden.astype(jnp.bfloat16)
-
-
-def hidden_of(own_rows, other_rows, weights):
-    parts, units = len(weights), weights[0].shape[0] // 4
-    count, width = own_rows.shape
+        weight_ref[...], rows, (((1,), (1,)), ((), ())), preferred_element_type=jnp.float32
+    )
+    units = weight_ref.shape[0] // 2
+    gate_val, up_val = products[:units], products[units:]
+    hidden = gate_val * jax.nn.sigmoid(1.702 * gate_val) * (up_val + 1.0)
+    out_ref[0] = hidden.astype(jnp.bfloat16)
+
+
+def hidden_of(row_blocks, weights):
+    units = weights.shape[0] // 4
+    count, width = row_blocks[0].shape
+    total = count * len(row_blocks)
     whole = pl.BlockSpec((count, width), lambda p: (0, 0))
     return pl.pallas_call(
         hidden_kernel,
         grid=(2,),
-        out_shape=jax.ShapeDtypeStruct((parts, 2, units, 2 * count), jnp.bfloat16),
-        in_specs=[whole, whole] + [pl.BlockSpec((2 * units, width), lambda p: (p, 0))] * len(weights),
-        out_specs=pl.BlockSpec((parts, 1, units, 2 * count), lambda p: (0, p, 0, 0)),
+        out_shape=jax.ShapeDtypeStruct((2, units, total), jnp.bfloat16),
+        in_specs=[whole] * len(row_blocks) + [pl.BlockSpec((2 * units, width), lambda p: (p, 0))],
+        out_specs=pl.BlockSpec((1, units, total), lambda p: (p, 0, 0)),
         compiler_params=pltpu.CompilerParams(vmem_limit_bytes=24 << 20),
         cost_estimate=pl.CostEstimate(
-            flops=16 * count * width * parts * units,
-            bytes_accessed=4 * (count * width + 2 * parts * units * width),
-            transcendentals=4 * parts * units * count,
+            flops=2 * total * weights.size,
+            bytes_accessed=2 * (total * width + weights.size + 2 * units * total),
+            transcendentals=2 * units * total,
         ),
-    )(own_rows, other_rows, *weights)
+    )(*row_blocks, weights)
 
 
 def attend(queries, key_vectors, head_value_vectors, head_sink_logits, previous):
@@ -266,22 +264,25 @@
     height = hidden_ref.shape[0] // len(device_at)
     rows = out_ref.shape[1]
     for p in range(2):
-        for c in range(2):
-            total = None
-            for q in range(2):
+        total = None
+        for q in range(2):
+            for c in range(2):
                 start = device_at[p, q, c] * height
                 for half, x in enumerate(chips_with[q]):
+                    f = 2 * x + c
                     term = lax.dot_general(
                         hidden_ref[start + half * units : start + (half + 1) * units, :],
-                        weight_ref[x * units : (x + 1) * units, :],
+                        weight_ref[f * units : (f + 1) * units, :],
                         ROW_CONTRACT,
                         preferred_element_type=jnp.float32,
                     )
                     total = term if total is None else total + term
-            for q in range(2):
+        for q in range(2):
+            for c in range(2):
                 f = device_at[p, q, c]
                 gate = gate_column(hidden_ref, f * height + 2 * units, rows)
-                out_ref[f] = (total[q * rows : (q + 1) * rows] * gate).astype(jnp.bfloat16)
+                block = total[(2 * q + c) * rows : (2 * q + c + 1) * rows]
+                out_ref[f] = (block * gate).astype(jnp.bfloat16)
 
 
 def gate_column(hidden_ref, start, rows):
@@ -293,27 +294,24 @@
     height = hidden_ref.shape[0] // len(device_at)
     rows = cotangent_ref.shape[0] // len(device_at)
     kept, chunk = out_ref.shape[1:]
-    order = [device_at[p, r, c] for p in range(2) for c in range(2) for r in range(2)]
+    order = [device_at[p, q, c] for p in range(2) for q in range(2) for c in range(2)]
     for i, f in enumerate(order):
         gate = gate_column(hidden_ref, f * height + 2 * units, rows)
         block = cotangent_ref[f * rows : (f + 1) * rows, :].astype(jnp.float32) * gate
         grad_ref[i * rows : (i + 1) * rows, :] = block.astype(jnp.bfloat16)
     for q in range(2):
         for half, x in enumerate(chips_with[q]):
-            total = None
-            for p in range(2):
-                for c in range(2):
+            for c in range(2):
+                total = None
+                for p in range(2):
                     start = device_at[p, q, c] * height + half * units
-                    first = 2 * (2 * p + c) * rows
                     term = jnp.dot(
                         hidden_ref[start : start + units, :],
-                        grad_ref[first : first + 2 * rows, :],
+                        grad_ref[4 * p * rows : 4 * (p + 1) * rows, :],
                         preferred_element_type=jnp.float32,
                     )
                     total = term if total is None else total + term
-            for c in range(2):
-                part = total[c * units // 2 : c * units // 2 + kept, :chunk]
-                out_ref[2 * x + c] = part.astype(jnp.bfloat16)
+                out_ref[2 * x + c] = total[:kept, :chunk].astype(jnp.bfloat16)
 
 
 IN_VMEM = pl.BlockSpec(memory_space=pltpu.VMEM)
@@ -375,18 +373,18 @@
     features = jnp.concatenate([router_weight.T, jnp.stack(gain_terms)], axis=0)
     features = swap_y_and_f(jnp.pad(features, ((0, 13), (0, wide - chunk))))
 
+    key_vectors, own_weights = lax.optimization_barrier((key_vectors, own_weights))
+    pair_weights = of_chip_pair(own_weights)
     previous = from_previous_block(key_vectors, head_value_vectors)
     out_columns = double_stack(out_weight.T[None], "z")
     previous, out_columns = lax.optimization_barrier((previous, out_columns))
     attended = attend(queries, key_vectors, head_value_vectors, head_sink_logits, previous)
-    attended, packed, own_weights = lax.optimization_barrier((attended, packed, own_weights))
-    pair_weights = of_chip_pair(own_weights)
+    attended, packed = lax.optimization_barrier((attended, packed))
     attended_all = to_all(attended, "y").reshape(side * tok_rows, attended.shape[1])
     while out_columns.shape[0] < depth:
         out_columns = double_stack(out_columns, "z")
     out_columns = out_columns.reshape(chunk, out_weight.shape[0])
     out_columns = jnp.pad(out_columns, ((0, wide - chunk), (0, 0)))
-    attended_all, features = lax.optimization_barrier((attended_all, features))
 
     partial_out = lax.dot_general(
         attended_all, out_columns, (((1,), (1,)), ((), ())), preferred_element_type=jnp.float32
@@ -423,38 +421,39 @@
     )
     own_gate = sums[:1].astype(jnp.bfloat16)
     other_rows = from_chip(expert_rows, Q_PARTNER)
-    expert_rows, pair_weights = lax.optimization_barrier((expert_rows, pair_weights))
-    core_weights = from_core(pair_weights)
+    core_rows = from_core(expert_rows)
+    far_rows = from_core(other_rows)
     cotangent_slots = local_call(
         slots_kernel,
         [jax.ShapeDtypeStruct((experts * capacity, wide), jnp.bfloat16)],
         (dest.T, jnp.pad(cotangent, ((0, 0), (0, wide - chunk)))),
         flops=2 * experts * capacity * tok_rows * wide,
     )[0].reshape(experts, capacity, wide)
-    other_rows, updated = lax.optimization_barrier((other_rows, updated))
-    hidden_units = hidden_of(expert_rows, other_rows, [pair_weights, core_weights])
+    hidden_units = hidden_of([expert_rows, core_rows, other_rows, far_rows], pair_weights)
     hidden_units, cotangent_slots = lax.optimization_barrier((hidden_units, cotangent_slots))
     cotangent_arrived = lax.all_to_all(cotangent_slots, SEQ, split_axis=0, concat_axis=0, tiled=True)
     rows_per_device = depth * capacity
-    hidden_units = ordered(hidden_units[0], hidden_units[1], core == 1, axis=1)
-    hidden_units = hidden_units.reshape(4 * units, 2 * rows_per_device)
-    hidden_units = jnp.where(
+    hidden_units = hidden_units.reshape(2 * units, 4 * rows_per_device)
+    blocks = [
+        hidden_units[:, i * rows_per_device : (i + 1) * rows_per_device] for i in range(4)
+    ]
+    hidden_units = ordered(
+        ordered(blocks[0], blocks[1], core == 1, axis=1),
+        ordered(blocks[2], blocks[3], core == 1, axis=1),
         in_second_q,
-        jnp.concatenate(
-            [hidden_units[:, rows_per_device:], hidden_units[:, :rows_per_device]], axis=1
-        ),
-        hidden_units,
-    )
-    gate_row = jnp.pad(own_gate, ((0, 15), (0, depth * capacity)))
+        axis=1,
+    )
+    gate_row = jnp.pad(own_gate, ((0, 15), (0, 3 * rows_per_device)))
     hidden_units = jnp.concatenate([hidden_units, gate_row], axis=0)
     gathered = lax.all_gather(hidden_units, "f", axis=0, tiled=True)
+    gathered, updated = lax.optimization_barrier((gathered, updated))
 
     device_at = {(P_OF[f // 2], Q_OF[f // 2], f % 2): f for f in range(8)}
     chips_with = [[x for x in range(4) if Q_OF[x] == q] for q in range(2)]
     down_rows = down_weight[0].reshape(side, hidden_part, chunk)
     down_rows = jnp.pad(down_rows, ((0, 0), *more_units)).reshape(side * units, chunk)
     expert_output = local_call(
-        functools.partial(down_kernel, device_at, chips_with, 2 * units),
+        functools.partial(down_kernel, device_at, chips_with, units),
         [jax.ShapeDtypeStruct((side, depth * capacity, chunk), jnp.bfloat16)],
         (gathered, down_rows),
         flops=2 * experts * capacity * down_weight.shape[1] * chunk,
@@ -465,7 +464,7 @@
     mixture = jnp.dot(placing, returned, preferred_element_type=jnp.float32)
     layer_output = (updated + mixture).astype(jnp.bfloat16)
     grad_local = pl.pallas_call(
-        functools.partial(grad_kernel, device_at, chips_with, 2 * units),
+        functools.partial(grad_kernel, device_at, chips_with, units),
         out_shape=jax.ShapeDtypeStruct((side, hidden_part, chunk), jnp.bfloat16),
         in_specs=[IN_VMEM] * 2,
         out_specs=IN_VMEM,

time: 251 us -> 246 us (0.980)
  the two profiles are of different devices: /device:TPU:16 before, /device:TPU:20 now
where the time goes in v3:
time: 246 us; the launch traced here: 245 us
  waiting for transfers between devices  82.3 us (33%)
  starting transfers between devices  75.5 us (31%)
  blocking collectives  37.3 us (15%)
  between operations  14.6 us (6%)
  local copies, waits for them, and re-layouts  14.4 us (6%)
  Pallas kernels  11.3 us (5%)
  other arithmetic  5.4 us (2%)
  matrix products  3.96 us (2%)
    all_to_all x1, blocking collectives, body(): lax.all_to_all(local_slots, SEQ, split_axis=0, concat_axis=0, tiled=True)  37.3 us
    ppermute x3, waiting for transfers between devices, swap_y_and_f(): return lax.ppermute(value, ('y', 'z', 'f'), pairs)  33.2 us
    all_to_all x1, waiting for transfers between devices, body(): lax.all_to_all(expert_output, SEQ, split_axis=0, concat_axis=0, tiled=True)  18.9 us
    ppermute x3, starting transfers between devices, double_stack(): other = lax.ppermute(stack, axis, [(i, i ^ step) for i in range(count)])  18.6 us
    ppermute x3, starting transfers between devices, swap_y_and_f(): return lax.ppermute(value, ('y', 'z', 'f'), pairs)  17.1 us
    all_to_all x1, waiting for transfers between devices, body(): lax.all_to_all(partial_out, 'f', split_axis=0, concat_axis=0, tiled=True)  14 us
    ppermute x1, waiting for transfers between devices, from_chip(): lax.ppermute(value, 'f', [(f, 2 * partner[f // 2] + f % 2) for f in range...  12 us
    all_to_all x1, starting transfers between devices, body(): lax.all_to_all(expert_output, SEQ, split_axis=0, concat_axis=0, tiled=True)  9.77 us
  transfers between devices with their start and end apart: 16, of which 7 were waited for; matrix products, arithmetic and copies ran while one was open for 3% of the time, Pallas kernels for 3%

profile of v3, /device:TPU:20, one launch (start us, length us, event | category | flops | bytes accessed | tf_op | source)
XLA Modules:
  0.0 244.8 jit_solution(17258546787555087426)
XLA Ops:
  7.2 3.2 %fusion.2 = bf16[384,2944]{1,0:T(8,128)(2,1)} fusion(bf16[180,2880]{1,0:T(8,128)(2,1)} %bitcast.61, bf16[180,2880]{1,0:T(8,128)(2,1)} %bitcast.62), kind=kLoop, calls=%fused_computation.4 | loop fusion | flops 9043968 | bytes 4334592 | tf_op jit(solution)/shard_map/concatenate | solution.py:361
  10.4 4.3 %collective-permute-start = (bf16[128,128]{0,1:T(8,128)(2,1)S(1)}, bf16[128,128]{0,1:T(8,128)(2,1)S(1)}, u32[]{:S(2)}, u32[]{:S(2)}) collective-permute-start(bf16[128,128]{0,1:T(8,128)(2,1)S(1)} %pad_maximum_fusion), channel_id=1, source_target_pairs={{0,8},{8,16},{16,24},{24,32},{32,40},{40,48},{48,56},{56,64},{64,7... | collective-permute-start | bytes 98312 | tf_op jit(solution)/shard_map/ppermute | solution.py:25
  14.7 4.3 %collective-permute-start.1 = (bf16[1,45,512]{2,1,0:T(8,128)(2,1)S(1)}, bf16[1,45,512]{2,1,0:T(8,128)(2,1)S(1)}, u32[]{:S(2)}, u32[]{:S(2)}) collective-permute-start(bf16[1,45,512]{2,1,0:T(8,128)(2,1)S(1)} %bitcast.68), channel_id=1, source_target_pairs={{0,8},{8,0},{16,24},{24,16},{32,40},{40,32},{48,56},{56,48},{1,9},... | collective-permute-start | bytes 138248 | tf_op jit(solution)/shard_map/ppermute | solution.py:48
  19.3 5.7 %collective-permute-start.2 = (bf16[128,384]{0,1:T(8,128)(2,1)S(1)}, bf16[128,384]{0,1:T(8,128)(2,1)S(1)}, u32[]{:S(2)}, u32[]{:S(2)}) collective-permute-start(bf16[128,384]{0,1:T(8,128)(2,1)S(1)} %fusion.18), channel_id=1, source_target_pairs={{0,0},{1,64},{2,128},{3,192},{4,256},{5,320},{6,384},{7,448},{8,8}... | collective-permute-start | bytes 294920 | tf_op jit(solution)/shard_map/ppermute | solution.py:37
  26.3 7.1 %collective-permute-done.2 = bf16[128,384]{0,1:T(8,128)(2,1)S(1)} collective-permute-done((bf16[128,384]{0,1:T(8,128)(2,1)S(1)}, bf16[128,384]{0,1:T(8,128)(2,1)S(1)}, u32[]{:S(2)}, u32[]{:S(2)}) %collective-permute-start.2) | collective-permute-done | bytes 98336 | tf_op jit(solution)/shard_map/ppermute | solution.py:37
  34.6 4.3 %all-to-all-start = ((bf16[8,128,512]{2,1,0:T(8,128)(2,1)}), bf16[8,128,512]{2,1,0:T(8,128)(2,1)S(1)}, u32[]{:S(2)}, u32[]{:S(2)}) async-start(bf16[8,128,512]{2,1,0:T(8,128)(2,1)} %broadcast_in_dim.18), calls=%async_computation | async-start | bytes 2097152 | tf_op jit(solution)/shard_map/all_to_all | solution.py:42
  38.9 7.3 %collective-permute-start.3 = (bf16[2,45,512]{2,1,0:T(8,128)(2,1)S(1)}, bf16[2,45,512]{2,1,0:T(8,128)(2,1)S(1)}, u32[]{:S(2)}, u32[]{:S(2)}) collective-permute-start(bf16[2,45,512]{2,1,0:T(8,128)(2,1)S(1)} %maximum_select_fusion.3), channel_id=1, source_target_pairs={{0,16},{8,24},{16,0},{24,8},{32,48},{40,56},{48,32},{56,40},{1,17}... | collective-permute-start | bytes 276488 | tf_op jit(solution)/shard_map/ppermute | solution.py:48
  46.2 3.3 %collective-permute-done.3 = bf16[2,45,512]{2,1,0:T(8,128)(2,1)S(1)} collective-permute-done((bf16[2,45,512]{2,1,0:T(8,128)(2,1)S(1)}, bf16[2,45,512]{2,1,0:T(8,128)(2,1)S(1)}, u32[]{:S(2)}, u32[]{:S(2)}) %collective-permute-start.3) | collective-permute-done | bytes 92192 | tf_op jit(solution)/shard_map/ppermute | solution.py:48
  49.5 7.0 %collective-permute-start.4 = (bf16[4,45,512]{2,1,0:T(8,128)(2,1)S(1)}, bf16[4,45,512]{2,1,0:T(8,128)(2,1)S(1)}, u32[]{:S(2)}, u32[]{:S(2)}) collective-permute-start(bf16[4,45,512]{2,1,0:T(8,128)(2,1)S(1)} %maximum_select_fusion.2), channel_id=1, source_target_pairs={{0,32},{8,40},{16,48},{24,56},{32,0},{40,8},{48,16},{56,24},{1,33}... | collective-permute-start | bytes 552968 | tf_op jit(solution)/shard_map/ppermute | solution.py:48
  56.7 6.9 %collective-permute-start.5 = (bf16[80,384]{1,0:T(8,128)(2,1)S(1)}, bf16[80,384]{1,0:T(8,128)(2,1)S(1)}, u32[]{:S(2)}, u32[]{:S(2)}) collective-permute-start(bf16[80,384]{1,0:T(8,128)(2,1)S(1)} %fusion.24), channel_id=1, source_target_pairs={{0,0},{1,64},{2,128},{3,192},{4,256},{5,320},{6,384},{7,448},{8,8}... | collective-permute-start | bytes 184328 | tf_op jit(solution)/shard_map/ppermute | solution.py:37
  63.8 1.6 convolution_convert_fusion
  65.4 6.5 %all-to-all-start.1 = ((bf16[8,128,384]{2,1,0:T(8,128)(2,1)}), bf16[8,128,384]{2,1,0:T(8,128)(2,1)S(1)}, u32[]{:S(2)}, u32[]{:S(2)}) async-start(bf16[8,128,384]{2,1,0:T(8,128)(2,1)} %bitcast.18), calls=%async_computation.1 | async-start | bytes 1572864 | tf_op jit(solution)/shard_map/all_to_all | solution.py:393
  72.3 14.0 %all-to-all-done.1.parts_ref = bf16[8,128,384]{2,1,0:T(8,128)(2,1)S(1)} async-done(((bf16[8,128,384]{2,1,0:T(8,128)(2,1)}), bf16[8,128,384]{2,1,0:T(8,128)(2,1)S(1)}, u32[]{:S(2)}, u32[]{:S(2)}) %all-to-all-start.1) | async-done | bytes 786464 | tf_op jit(solution)/shard_map/all_to_all | solution.py:393
  87.2 37.3 %all_to_all.25 = bf16[64,16,384]{2,1,0:T(8,128)(2,1)S(1)} all-to-all(bf16[64,16,384]{2,1,0:T(8,128)(2,1)S(1)} %bitcast.59), channel_id=1, replica_groups=mesh['y'=8,'z'=8,'f'=8] {'y','z'}, dimensions={0} | all-to-all | bytes 1572864 | tf_op jit(solution)/shard_map/all_to_all | solution.py:406
  125.1 3.1 %collective-permute-start.7 = (bf16[128,2944]{1,0:T(8,128)(2,1)S(1)}, bf16[128,2944]{1,0:T(8,128)(2,1)S(1)}, u32[]{:S(2)}, u32[]{:S(2)}) collective-permute-start(bf16[128,2944]{1,0:T(8,128)(2,1)S(1)} %get-tuple-element.26.refs_0_), channel_id=1, source_target_pairs={{0,2},{1,3},{2,0},{3,1},{4,6},{5,7},{6,4},{7,5},{8,10},{9,11},{10,... | collective-permute-start | bytes 2261000 | tf_op jit(solution)/shard_map/ppermute | solution.py:71
  128.2 1.9 collective-permute-start.6
  130.1 12.0 %collective-permute-done.7.refs_2_ = bf16[128,2944]{1,0:T(8,128)(2,1)S(1)} collective-permute-done((bf16[128,2944]{1,0:T(8,128)(2,1)S(1)}, bf16[128,2944]{1,0:T(8,128)(2,1)S(1)}, u32[]{:S(2)}, u32[]{:S(2)}) %collective-permute-start.7) | collective-permute-done | bytes 753696 | tf_op jit(solution)/shard_map/ppermute | solution.py:71
  142.1 1.9 collective-permute-start.8
  144.2 1.3 shard_map.143
  146.3 2.3 copy-done.5
  148.5 2.9 %shard_map.142 = bf16[2,192,512]{2,1,0:T(8,128)(2,1)S(1)} custom-call(bf16[128,2944]{1,0:T(8,128)(2,1)S(1)} %get-tuple-element.26.refs_0_, bf16[128,2944]{1,0:T(8,128)(2,1)S(1)} %collective-permute-done.6.refs_1_, bf16[128,2944]{1,0:T(8,128)(2,1)S(1)} %collective-permute-done.7.refs_2_, bf16[128,2944]{1,0:T(8,128)(2,1)S(1)} %collective-permute-done.8.refs_3_, ...), custom_call_target="tpu_custom_call" | custom-call | flops 2315255808 | bytes 7929856 | tf_op jit(solution)/shard_map/pallas_call | solution.py:102
  152.5 8.1 %all-to-all-start.3 = ((bf16[64,16,384]{2,1,0:T(8,128)(2,1)}), bf16[64,16,384]{2,1,0:T(8,128)(2,1)}, u32[]{:S(2)}, u32[]{:S(2)}) async-start(bf16[64,16,384]{2,1,0:T(8,128)(2,1)} %bitcast.24), calls=%async_computation.3 | async-start | bytes 1572864 | tf_op jit(solution)/shard_map/all_to_all | solution.py:434
  160.6 4.5 %collective-permute-start.9 = (f32[128,384]{1,0:T(8,128)S(1)}, f32[128,384]{1,0:T(8,128)S(1)}, u32[]{:S(2)}, u32[]{:S(2)}) collective-permute-start(f32[128,384]{1,0:T(8,128)S(1)} %get-tuple-element.30), channel_id=1, source_target_pairs={{0,0},{1,64},{2,128},{3,192},{4,256},{5,320},{6,384},{7,448},{8,8}... | collective-permute-start | bytes 589832 | tf_op jit(solution)/shard_map/ppermute | solution.py:37
  166.7 26.2 %collective-permute-done.9 = f32[128,384]{1,0:T(8,128)S(1)} collective-permute-done((f32[128,384]{1,0:T(8,128)S(1)}, f32[128,384]{1,0:T(8,128)S(1)}, u32[]{:S(2)}, u32[]{:S(2)}) %collective-permute-start.9) | collective-permute-done | bytes 196640 | tf_op jit(solution)/shard_map/ppermute | solution.py:37
  193.5 1.9 copy-done
  195.5 1.3 copy-done.2
  196.7 2.4 shard_map.144
  200.1 9.8 %all-to-all-start.4 = ((bf16[64,16,360]{2,1,0:T(8,128)(2,1)}), bf16[64,16,360]{2,1,0:T(8,128)(2,1)}, u32[]{:S(2)}, u32[]{:S(2)}) async-start(bf16[64,16,360]{2,1,0:T(8,128)(2,1)} %bitcast.55), calls=%async_computation.4 | async-start | bytes 1572864 | tf_op jit(solution)/shard_map/all_to_all | solution.py:462
  210.2 3.3 %shard_map.145 = bf16[8,180,360]{2,1,0:T(8,128)(2,1)S(1)} custom-call(bf16[3200,512]{1,0:T(8,128)(2,1)S(1)} %copy-done.1, bf16[1024,384]{1,0:T(8,128)(2,1)} %bitcast.29.cotangent_ref), custom_call_target="tpu_custom_call" | custom-call | flops 1207959552 | bytes 4849664 | tf_op jit(solution)/shard_map/pallas_call | solution.py:466
  214.5 2.3 reshape.164
  216.8 18.9 %all-to-all-done.4 = bf16[64,16,360]{2,1,0:T(8,128)(2,1)} async-done(((bf16[64,16,360]{2,1,0:T(8,128)(2,1)}), bf16[64,16,360]{2,1,0:T(8,128)(2,1)}, u32[]{:S(2)}, u32[]{:S(2)}) %all-to-all-start.4) | async-done | bytes 737312 | tf_op jit(solution)/shard_map/all_to_all | solution.py:462
  235.7 1.4 fusion.42
  (98 shorter events, 12.0 us)
Async XLA Ops:
  7.2 3.3 %copy-start.12 = (bf16[128,64]{0,1:T(8,128)(2,1)S(1)}, bf16[128,64]{0,1:T(8,128)(2,1)}, u32[]{:S(2)}) copy-start(bf16[128,64]{0,1:T(8,128)(2,1)} %param.14) | copy-start | bytes 49156
  7.2 3.3 %copy-start.16 = (bf16[128,64]{0,1:T(8,128)(2,1)S(1)}, bf16[128,64]{0,1:T(8,128)(2,1)}, u32[]{:S(2)}) copy-start(bf16[128,64]{0,1:T(8,128)(2,1)} %param.15) | copy-start | bytes 49156
  7.2 7.6 %copy-start.14 = (bf16[512,45]{0,1:T(8,128)(2,1)S(1)}, bf16[512,45]{0,1:T(8,128)(2,1)}, u32[]{:S(2)}) copy-start(bf16[512,45]{0,1:T(8,128)(2,1)} %param.17) | copy-start | bytes 138244
  7.2 11.8 %copy-start.15 = (s32[128,4]{0,1:T(4,128)S(1)}, s32[128,4]{0,1:T(4,128)}, u32[]{:S(2)}) copy-start(s32[128,4]{0,1:T(4,128)} %param.21) | copy-start | bytes 6148
  7.2 12.1 %copy-start.10 = (bf16[128,360]{0,1:T(8,128)(2,1)S(1)}, bf16[128,360]{0,1:T(8,128)(2,1)}, u32[]{:S(2)}) copy-start(bf16[128,360]{0,1:T(8,128)(2,1)} %param.18) | copy-start | bytes 276484
  7.2 18.0 %copy-start.9 = (bf16[128,512]{1,0:T(8,128)(2,1)S(1)}, bf16[128,512]{1,0:T(8,128)(2,1)}, u32[]{:S(2)}) copy-start(bf16[128,512]{1,0:T(8,128)(2,1)} %param.13) | copy-start | bytes 393220
  7.2 18.5 %copy-start.17 = (f32[8]{0:T(128)S(1)}, f32[8]{0:T(128)}, u32[]{:S(2)}) copy-start(f32[8]{0:T(128)} %param.16) | copy-start | bytes 100
  10.4 14.9 %collective-permute-start = (bf16[128,128]{0,1:T(8,128)(2,1)S(1)}, bf16[128,128]{0,1:T(8,128)(2,1)S(1)}, u32[]{:S(2)}, u32[]{:S(2)}) collective-permute-start(bf16[128,128]{0,1:T(8,128)(2,1)S(1)} %pad_maximum_fusion), channel_id=1, source_target_pairs={{0,8},{8,16},{16,24},{24,32},{32,40},{40,48},{48,56},{56,64},{64,7... | collective-permute-start | bytes 98312 | tf_op jit(solution)/shard_map/ppermute | solution.py:25
  14.7 10.6 %collective-permute-start.1 = (bf16[1,45,512]{2,1,0:T(8,128)(2,1)S(1)}, bf16[1,45,512]{2,1,0:T(8,128)(2,1)S(1)}, u32[]{:S(2)}, u32[]{:S(2)}) collective-permute-start(bf16[1,45,512]{2,1,0:T(8,128)(2,1)S(1)} %bitcast.68), channel_id=1, source_target_pairs={{0,8},{8,0},{16,24},{24,16},{32,40},{40,32},{48,56},{56,48},{1,9},... | collective-permute-start | bytes 138248 | tf_op jit(solution)/shard_map/ppermute | solution.py:48
  19.3 14.1 %collective-permute-start.2 = (bf16[128,384]{0,1:T(8,128)(2,1)S(1)}, bf16[128,384]{0,1:T(8,128)(2,1)S(1)}, u32[]{:S(2)}, u32[]{:S(2)}) collective-permute-start(bf16[128,384]{0,1:T(8,128)(2,1)S(1)} %fusion.18), channel_id=1, source_target_pairs={{0,0},{1,64},{2,128},{3,192},{4,256},{5,320},{6,384},{7,448},{8,8}... | collective-permute-start | bytes 294920 | tf_op jit(solution)/shard_map/ppermute | solution.py:37
  34.6 22.0 %copy-start.18 = (f32[360]{0:T(512)S(1)}, f32[360]{0:T(512)}, u32[]{:S(2)}) copy-start(f32[360]{0:T(512)} %param.19) | copy-start | bytes 4324
  34.6 22.0 %copy-start.13 = (bf16[360,64]{0,1:T(8,128)(2,1)S(1)}, bf16[360,64]{0,1:T(8,128)(2,1)}, u32[]{:S(2)}) copy-start(bf16[360,64]{0,1:T(8,128)(2,1)} %param.20) | copy-start | bytes 138244
  34.6 29.2 %all-to-all-start = ((bf16[8,128,512]{2,1,0:T(8,128)(2,1)}), bf16[8,128,512]{2,1,0:T(8,128)(2,1)S(1)}, u32[]{:S(2)}, u32[]{:S(2)}) async-start(bf16[8,128,512]{2,1,0:T(8,128)(2,1)} %broadcast_in_dim.18), calls=%async_computation | async-start | bytes 2097152 | tf_op jit(solution)/shard_map/all_to_all | solution.py:42
  38.9 106.6 %all-gather.3.cloned.1.call-start = ((), (), s32[]{:S(2)}) async-start(), calls=%async_computation.5 | async-start | bytes 6782976 | tf_op jit(solution)/shard_map/all_gather | solution.py:76
  38.9 10.6 %collective-permute-start.3 = (bf16[2,45,512]{2,1,0:T(8,128)(2,1)S(1)}, bf16[2,45,512]{2,1,0:T(8,128)(2,1)S(1)}, u32[]{:S(2)}, u32[]{:S(2)}) collective-permute-start(bf16[2,45,512]{2,1,0:T(8,128)(2,1)S(1)} %maximum_select_fusion.3), channel_id=1, source_target_pairs={{0,16},{8,24},{16,0},{24,8},{32,48},{40,56},{48,32},{56,40},{1,17}... | collective-permute-start | bytes 276488 | tf_op jit(solution)/shard_map/ppermute | solution.py:48
  49.5 14.0 %collective-permute-start.4 = (bf16[4,45,512]{2,1,0:T(8,128)(2,1)S(1)}, bf16[4,45,512]{2,1,0:T(8,128)(2,1)S(1)}, u32[]{:S(2)}, u32[]{:S(2)}) collective-permute-start(bf16[4,45,512]{2,1,0:T(8,128)(2,1)S(1)} %maximum_select_fusion.2), channel_id=1, source_target_pairs={{0,32},{8,40},{16,48},{24,56},{32,0},{40,8},{48,16},{56,24},{1,33}... | collective-permute-start | bytes 552968 | tf_op jit(solution)/shard_map/ppermute | solution.py:48
  56.7 15.6 %collective-permute-start.5 = (bf16[80,384]{1,0:T(8,128)(2,1)S(1)}, bf16[80,384]{1,0:T(8,128)(2,1)S(1)}, u32[]{:S(2)}, u32[]{:S(2)}) collective-permute-start(bf16[80,384]{1,0:T(8,128)(2,1)S(1)} %fusion.24), channel_id=1, source_target_pairs={{0,0},{1,64},{2,128},{3,192},{4,256},{5,320},{6,384},{7,448},{8,8}... | collective-permute-start | bytes 184328 | tf_op jit(solution)/shard_map/ppermute | solution.py:37
  65.4 78.7 %copy-start.11 = (bf16[128,360]{0,1:T(8,128)(2,1)S(1)}, bf16[128,360]{0,1:T(8,128)(2,1)}, u32[]{:S(2)}) copy-start(bf16[128,360]{0,1:T(8,128)(2,1)} %param.25) | copy-start | bytes 276484
  65.4 20.9 %all-to-all-start.1 = ((bf16[8,128,384]{2,1,0:T(8,128)(2,1)}), bf16[8,128,384]{2,1,0:T(8,128)(2,1)S(1)}, u32[]{:S(2)}, u32[]{:S(2)}) async-start(bf16[8,128,384]{2,1,0:T(8,128)(2,1)} %bitcast.18), calls=%async_computation.1 | async-start | bytes 1572864 | tf_op jit(solution)/shard_map/all_to_all | solution.py:393
  71.9 121.0 %all-gather.5.cloned.1.call-start = ((), (), s32[]{:S(2)}) async-start(), calls=%async_computation.6 | async-start | bytes 3686400 | tf_op jit(solution)/shard_map/all_gather | solution.py:448
  125.1 17.1 %collective-permute-start.7 = (bf16[128,2944]{1,0:T(8,128)(2,1)S(1)}, bf16[128,2944]{1,0:T(8,128)(2,1)S(1)}, u32[]{:S(2)}, u32[]{:S(2)}) collective-permute-start(bf16[128,2944]{1,0:T(8,128)(2,1)S(1)} %get-tuple-element.26.refs_0_), channel_id=1, source_target_pairs={{0,2},{1,3},{2,0},{3,1},{4,6},{5,7},{6,4},{7,5},{8,10},{9,11},{10,... | collective-permute-start | bytes 2261000 | tf_op jit(solution)/shard_map/ppermute | solution.py:71
  128.2 17.3 %collective-permute-start.6 = (bf16[128,2944]{1,0:T(8,128)(2,1)S(1)}, bf16[128,2944]{1,0:T(8,128)(2,1)S(1)}, u32[]{:S(2)}, u32[]{:S(2)}) collective-permute-start(bf16[128,2944]{1,0:T(8,128)(2,1)S(1)} %get-tuple-element.26.refs_0_), channel_id=1, source_target_pairs={{0,1},{1,0},{2,3},{3,2},{4,5},{5,4},{6,7},{7,6},{8,9},{9,8},{10,11... | collective-permute-start | bytes 2261000 | tf_op jit(solution)/shard_map/ppermute | solution.py:67
  142.1 4.1 %collective-permute-start.8 = (bf16[128,2944]{1,0:T(8,128)(2,1)S(1)}, bf16[128,2944]{1,0:T(8,128)(2,1)S(1)}, u32[]{:S(2)}, u32[]{:S(2)}) collective-permute-start(bf16[128,2944]{1,0:T(8,128)(2,1)S(1)} %collective-permute-done.7.refs_2_), channel_id=1, source_target_pairs={{0,1},{1,0},{2,3},{3,2},{4,5},{5,4},{6,7},{7,6},{8,9},{9,8},{10,11... | collective-permute-start | bytes 2261000 | tf_op jit(solution)/shard_map/ppermute | solution.py:67
  146.3 2.3 copy-start.5
  151.5 13.7 %copy-start.6 = (bf16[1,1440,360]{2,1,0:T(8,128)(2,1)S(1)}, bf16[1,1440,360]{2,1,0:T(8,128)(2,1)}, u32[]{:S(2)}) copy-start(bf16[1,1440,360]{2,1,0:T(8,128)(2,1)} %param.24) | copy-start | bytes 3110404
  152.5 47.5 %all-to-all-start.3 = ((bf16[64,16,384]{2,1,0:T(8,128)(2,1)}), bf16[64,16,384]{2,1,0:T(8,128)(2,1)}, u32[]{:S(2)}, u32[]{:S(2)}) async-start(bf16[64,16,384]{2,1,0:T(8,128)(2,1)} %bitcast.24), calls=%async_computation.3 | async-start | bytes 1572864 | tf_op jit(solution)/shard_map/all_to_all | solution.py:434
  160.6 32.2 %collective-permute-start.9 = (f32[128,384]{1,0:T(8,128)S(1)}, f32[128,384]{1,0:T(8,128)S(1)}, u32[]{:S(2)}, u32[]{:S(2)}) collective-permute-start(f32[128,384]{1,0:T(8,128)S(1)} %get-tuple-element.30), channel_id=1, source_target_pairs={{0,0},{1,64},{2,128},{3,192},{4,256},{5,320},{6,384},{7,448},{8,8}... | collective-permute-start | bytes 589832 | tf_op jit(solution)/shard_map/ppermute | solution.py:37
  193.5 1.9 copy-start
  195.4 1.3 copy-start.2
  196.7 13.5 %copy-start.1 = (bf16[3200,512]{1,0:T(8,128)(2,1)S(1)}, bf16[3200,512]{1,0:T(8,128)(2,1)}, u32[]{:S(2)}) copy-start(bf16[3200,512]{1,0:T(8,128)(2,1)} %all-gather.5.cloned.1.call-done.hidden_ref) | copy-start | bytes 9830404
  200.1 35.6 %all-to-all-start.4 = ((bf16[64,16,360]{2,1,0:T(8,128)(2,1)}), bf16[64,16,360]{2,1,0:T(8,128)(2,1)}, u32[]{:S(2)}, u32[]{:S(2)}) async-start(bf16[64,16,360]{2,1,0:T(8,128)(2,1)} %bitcast.55), calls=%async_computation.4 | async-start | bytes 1572864 | tf_op jit(solution)/shard_map/all_to_all | solution.py:462
  214.5 22.6 %copy-start.8 = (f32[128,384]{1,0:T(8,128)S(1)}, f32[128,384]{1,0:T(8,128)}, u32[]{:S(2)}) copy-start(f32[128,384]{1,0:T(8,128)} %copy-done.7) | copy-start | bytes 589828
  (3 other events, 2.6 us)
Sparse Core Ops, SparseCore 0:
  46.4 76.4 all-gather.2
  152.7 28.2 all-gather.4

commit v4 on v3

--- a/solution.py
+++ b/solution.py
@@ -405,7 +405,7 @@
     local_slots = local_slots.reshape(experts, capacity, wide)
     arrived = lax.all_to_all(local_slots, SEQ, split_axis=0, concat_axis=0, tiled=True)
 
-    updated = swap_y_and_f(updated_here)[:, :chunk]
+    updated = swap_y_and_f(updated_here.astype(jnp.bfloat16))[:, :chunk].astype(jnp.float32)
     dest = places_of(expert_ids, experts, capacity)
     slot_row = jnp.arange(experts * capacity, dtype=jnp.int32)
     placing = jnp.any(dest[:, :, None] == slot_row, axis=1).astype(jnp.bfloat16)

time: 246 us -> 241 us (0.980)
  the two profiles are of different devices: /device:TPU:20 before, /device:TPU:16 now
where the time goes in v4:
time: 241 us; the launch traced here: 240 us
  starting transfers between devices  77.5 us (32%)
  waiting for transfers between devices  76.9 us (32%)
  blocking collectives  34.9 us (14%)
  between operations  14.6 us (6%)
  local copies, waits for them, and re-layouts  13.7 us (6%)
  Pallas kernels  12.4 us (5%)
  other arithmetic  6.1 us (3%)
  matrix products  3.95 us (2%)
    all_to_all x1, blocking collectives, body(): lax.all_to_all(local_slots, SEQ, split_axis=0, concat_axis=0, tiled=True)  34.9 us
    ppermute x3, waiting for transfers between devices, swap_y_and_f(): return lax.ppermute(value, ('y', 'z', 'f'), pairs)  22.2 us
    ppermute x3, starting transfers between devices, double_stack(): other = lax.ppermute(stack, axis, [(i, i ^ step) for i in range(count)])  18.9 us
    all_to_all x1, waiting for transfers between devices, body(): lax.all_to_all(expert_output, SEQ, split_axis=0, concat_axis=0, tiled=True)  17.5 us
    all_to_all x1, waiting for transfers between devices, body(): lax.all_to_all(partial_out, 'f', split_axis=0, concat_axis=0, tiled=True)  16.9 us
    all_to_all x1, starting transfers between devices, body(): lax.all_to_all(expert_output, SEQ, split_axis=0, concat_axis=0, tiled=True)  13.3 us
    all_to_all x1, starting transfers between devices, to_all(): return lax.all_to_all(copies, axis, split_axis=0, concat_axis=0, tiled=True)  11.7 us
    ppermute x1, waiting for transfers between devices, from_chip(): lax.ppermute(value, 'f', [(f, 2 * partner[f // 2] + f % 2) for f in range...  11.1 us
  transfers between devices with their start and end apart: 16, of which 10 were waited for; matrix products, arithmetic and copies ran while one was open for 4% of the time, Pallas kernels for 3%

profile of v4, /device:TPU:16, one launch (start us, length us, event | category | flops | bytes accessed | tf_op | source)
XLA Modules:
  0.0 240.0 jit_solution(2017029918953435384)
XLA Ops:
  7.2 3.2 %fusion.2 = bf16[384,2944]{1,0:T(8,128)(2,1)} fusion(bf16[180,2880]{1,0:T(8,128)(2,1)} %bitcast.60, bf16[180,2880]{1,0:T(8,128)(2,1)} %bitcast.61), kind=kLoop, calls=%fused_computation.4 | loop fusion | flops 9043968 | bytes 4334592 | tf_op jit(solution)/shard_map/concatenate | solution.py:361
  10.5 4.3 %collective-permute-start = (bf16[128,128]{0,1:T(8,128)(2,1)S(1)}, bf16[128,128]{0,1:T(8,128)(2,1)S(1)}, u32[]{:S(2)}, u32[]{:S(2)}) collective-permute-start(bf16[128,128]{0,1:T(8,128)(2,1)S(1)} %pad_maximum_fusion), channel_id=1, source_target_pairs={{0,8},{8,16},{16,24},{24,32},{32,40},{40,48},{48,56},{56,64},{64,7... | collective-permute-start | bytes 98312 | tf_op jit(solution)/shard_map/ppermute | solution.py:25
  14.8 4.3 %collective-permute-start.1 = (bf16[1,45,512]{2,1,0:T(8,128)(2,1)S(1)}, bf16[1,45,512]{2,1,0:T(8,128)(2,1)S(1)}, u32[]{:S(2)}, u32[]{:S(2)}) collective-permute-start(bf16[1,45,512]{2,1,0:T(8,128)(2,1)S(1)} %bitcast.66), channel_id=1, source_target_pairs={{0,8},{8,0},{16,24},{24,16},{32,40},{40,32},{48,56},{56,48},{1,9},... | collective-permute-start | bytes 138248 | tf_op jit(solution)/shard_map/ppermute | solution.py:48
  19.3 3.2 %collective-permute-start.2 = (bf16[128,384]{0,1:T(8,128)(2,1)S(1)}, bf16[128,384]{0,1:T(8,128)(2,1)S(1)}, u32[]{:S(2)}, u32[]{:S(2)}) collective-permute-start(bf16[128,384]{0,1:T(8,128)(2,1)S(1)} %fusion.18), channel_id=1, source_target_pairs={{0,0},{1,64},{2,128},{3,192},{4,256},{5,320},{6,384},{7,448},{8,8}... | collective-permute-start | bytes 294920 | tf_op jit(solution)/shard_map/ppermute | solution.py:37
  24.2 4.2 %collective-permute-done.2 = bf16[128,384]{0,1:T(8,128)(2,1)S(1)} collective-permute-done((bf16[128,384]{0,1:T(8,128)(2,1)S(1)}, bf16[128,384]{0,1:T(8,128)(2,1)S(1)}, u32[]{:S(2)}, u32[]{:S(2)}) %collective-permute-start.2) | collective-permute-done | bytes 98336 | tf_op jit(solution)/shard_map/ppermute | solution.py:37
  29.6 11.7 %all-to-all-start = ((bf16[8,128,512]{2,1,0:T(8,128)(2,1)}), bf16[8,128,512]{2,1,0:T(8,128)(2,1)S(1)}, u32[]{:S(2)}, u32[]{:S(2)}) async-start(bf16[8,128,512]{2,1,0:T(8,128)(2,1)} %broadcast_in_dim.18), calls=%async_computation | async-start | bytes 2097152 | tf_op jit(solution)/shard_map/all_to_all | solution.py:42
  41.3 7.3 %collective-permute-start.3 = (bf16[2,45,512]{2,1,0:T(8,128)(2,1)S(1)}, bf16[2,45,512]{2,1,0:T(8,128)(2,1)S(1)}, u32[]{:S(2)}, u32[]{:S(2)}) collective-permute-start(bf16[2,45,512]{2,1,0:T(8,128)(2,1)S(1)} %maximum_select_fusion.3), channel_id=1, source_target_pairs={{0,16},{8,24},{16,0},{24,8},{32,48},{40,56},{48,32},{56,40},{1,17}... | collective-permute-start | bytes 276488 | tf_op jit(solution)/shard_map/ppermute | solution.py:48
  48.6 3.0 %collective-permute-done.3 = bf16[2,45,512]{2,1,0:T(8,128)(2,1)S(1)} collective-permute-done((bf16[2,45,512]{2,1,0:T(8,128)(2,1)S(1)}, bf16[2,45,512]{2,1,0:T(8,128)(2,1)S(1)}, u32[]{:S(2)}, u32[]{:S(2)}) %collective-permute-start.3) | collective-permute-done | bytes 92192 | tf_op jit(solution)/shard_map/ppermute | solution.py:48
  51.6 7.3 %collective-permute-start.4 = (bf16[4,45,512]{2,1,0:T(8,128)(2,1)S(1)}, bf16[4,45,512]{2,1,0:T(8,128)(2,1)S(1)}, u32[]{:S(2)}, u32[]{:S(2)}) collective-permute-start(bf16[4,45,512]{2,1,0:T(8,128)(2,1)S(1)} %maximum_select_fusion.2), channel_id=1, source_target_pairs={{0,32},{8,40},{16,48},{24,56},{32,0},{40,8},{48,16},{56,24},{1,33}... | collective-permute-start | bytes 552968 | tf_op jit(solution)/shard_map/ppermute | solution.py:48
  59.0 1.9 collective-permute-start.5
  61.0 2.6 %collective-permute-done.4 = bf16[4,45,512]{2,1,0:T(8,128)(2,1)S(1)} collective-permute-done((bf16[4,45,512]{2,1,0:T(8,128)(2,1)S(1)}, bf16[4,45,512]{2,1,0:T(8,128)(2,1)S(1)}, u32[]{:S(2)}, u32[]{:S(2)}) %collective-permute-start.4) | collective-permute-done | bytes 184352 | tf_op jit(solution)/shard_map/ppermute | solution.py:48
  63.8 1.6 convolution_convert_fusion
  65.4 6.0 %all-to-all-start.1 = ((bf16[8,128,384]{2,1,0:T(8,128)(2,1)}), bf16[8,128,384]{2,1,0:T(8,128)(2,1)S(1)}, u32[]{:S(2)}, u32[]{:S(2)}) async-start(bf16[8,128,384]{2,1,0:T(8,128)(2,1)} %bitcast.18), calls=%async_computation.1 | async-start | bytes 1572864 | tf_op jit(solution)/shard_map/all_to_all | solution.py:393
  71.8 16.9 %all-to-all-done.1.parts_ref = bf16[8,128,384]{2,1,0:T(8,128)(2,1)S(1)} async-done(((bf16[8,128,384]{2,1,0:T(8,128)(2,1)}), bf16[8,128,384]{2,1,0:T(8,128)(2,1)S(1)}, u32[]{:S(2)}, u32[]{:S(2)}) %all-to-all-start.1) | async-done | bytes 786464 | tf_op jit(solution)/shard_map/all_to_all | solution.py:393
  89.6 34.9 %all_to_all.25 = bf16[64,16,384]{2,1,0:T(8,128)(2,1)S(1)} all-to-all(bf16[64,16,384]{2,1,0:T(8,128)(2,1)S(1)} %bitcast.58), channel_id=1, replica_groups=mesh['y'=8,'z'=8,'f'=8] {'y','z'}, dimensions={0} | all-to-all | bytes 1572864 | tf_op jit(solution)/shard_map/all_to_all | solution.py:406
  125.1 3.4 %collective-permute-start.7 = (bf16[128,2944]{1,0:T(8,128)(2,1)S(1)}, bf16[128,2944]{1,0:T(8,128)(2,1)S(1)}, u32[]{:S(2)}, u32[]{:S(2)}) collective-permute-start(bf16[128,2944]{1,0:T(8,128)(2,1)S(1)} %get-tuple-element.26.refs_0_), channel_id=1, source_target_pairs={{0,2},{1,3},{2,0},{3,1},{4,6},{5,7},{6,4},{7,5},{8,10},{9,11},{10,... | collective-permute-start | bytes 2261000 | tf_op jit(solution)/shard_map/ppermute | solution.py:71
  128.5 1.9 collective-permute-start.6
  130.4 11.1 %collective-permute-done.7.refs_2_ = bf16[128,2944]{1,0:T(8,128)(2,1)S(1)} collective-permute-done((bf16[128,2944]{1,0:T(8,128)(2,1)S(1)}, bf16[128,2944]{1,0:T(8,128)(2,1)S(1)}, u32[]{:S(2)}, u32[]{:S(2)}) %collective-permute-start.7) | collective-permute-done | bytes 753696 | tf_op jit(solution)/shard_map/ppermute | solution.py:71
  141.6 1.9 collective-permute-start.8
  145.8 2.3 copy-done.5
  148.1 4.0 %shard_map.142 = bf16[2,192,512]{2,1,0:T(8,128)(2,1)S(1)} custom-call(bf16[128,2944]{1,0:T(8,128)(2,1)S(1)} %get-tuple-element.26.refs_0_, bf16[128,2944]{1,0:T(8,128)(2,1)S(1)} %collective-permute-done.6.refs_1_, bf16[128,2944]{1,0:T(8,128)(2,1)S(1)} %collective-permute-done.7.refs_2_, bf16[128,2944]{1,0:T(8,128)(2,1)} %collective-permute-done.8.refs_3_, ...), custom_call_target="tpu_custom_call" | custom-call | flops 2315255808 | bytes 7929856 | tf_op jit(solution)/shard_map/pallas_call | solution.py:102
  153.2 7.6 %all-to-all-start.3 = ((bf16[64,16,384]{2,1,0:T(8,128)(2,1)}), bf16[64,16,384]{2,1,0:T(8,128)(2,1)}, u32[]{:S(2)}, u32[]{:S(2)}) async-start(bf16[64,16,384]{2,1,0:T(8,128)(2,1)} %bitcast.24), calls=%async_computation.3 | async-start | bytes 1572864 | tf_op jit(solution)/shard_map/all_to_all | solution.py:434
  160.9 3.3 %collective-permute-start.9 = (bf16[128,384]{1,0:T(8,128)(2,1)S(1)}, bf16[128,384]{1,0:T(8,128)(2,1)S(1)}, u32[]{:S(2)}, u32[]{:S(2)}) collective-permute-start(bf16[128,384]{1,0:T(8,128)(2,1)S(1)} %convert_element_type.92), channel_id=1, source_target_pairs={{0,0},{1,64},{2,128},{3,192},{4,256},{5,320},{6,384},{7,448},{8,8}... | collective-permute-start | bytes 294920 | tf_op jit(solution)/shard_map/ppermute | solution.py:37
  165.7 18.0 %collective-permute-done.9 = bf16[128,384]{1,0:T(8,128)(2,1)S(1)} collective-permute-done((bf16[128,384]{1,0:T(8,128)(2,1)S(1)}, bf16[128,384]{1,0:T(8,128)(2,1)S(1)}, u32[]{:S(2)}, u32[]{:S(2)}) %collective-permute-start.9) | collective-permute-done | bytes 98336 | tf_op jit(solution)/shard_map/ppermute | solution.py:37
  183.7 2.3 all-gather.5.cloned.1.call-done.hidden_ref
  186.0 1.9 copy-done
  189.2 2.4 %shard_map.144 = bf16[8,128,360]{2,1,0:T(8,128)(2,1)S(1)} custom-call(bf16[3200,512]{1,0:T(8,128)(2,1)S(1)} %copy-done, bf16[1536,360]{1,0:T(8,128)(2,1)S(1)} %bitcast.53), custom_call_target="tpu_custom_call" | custom-call | flops 1061683200 | bytes 5120000 | tf_op jit(solution)/shard_map/pallas_call | solution.py:322
  192.6 13.3 %all-to-all-start.4 = ((bf16[64,16,360]{2,1,0:T(8,128)(2,1)}), bf16[64,16,360]{2,1,0:T(8,128)(2,1)}, u32[]{:S(2)}, u32[]{:S(2)}) async-start(bf16[64,16,360]{2,1,0:T(8,128)(2,1)} %bitcast.54), calls=%async_computation.4 | async-start | bytes 1572864 | tf_op jit(solution)/shard_map/all_to_all | solution.py:462
  206.9 3.2 %shard_map.145 = bf16[8,180,360]{2,1,0:T(8,128)(2,1)S(1)} custom-call(bf16[3200,512]{1,0:T(8,128)(2,1)S(1)} %copy-done.1, bf16[1024,384]{1,0:T(8,128)(2,1)} %bitcast.29.cotangent_ref), custom_call_target="tpu_custom_call" | custom-call | flops 1207959552 | bytes 4849664 | tf_op jit(solution)/shard_map/pallas_call | solution.py:466
  211.2 2.3 reshape.164
  213.5 17.5 %all-to-all-done.4 = bf16[64,16,360]{2,1,0:T(8,128)(2,1)} async-done(((bf16[64,16,360]{2,1,0:T(8,128)(2,1)}), bf16[64,16,360]{2,1,0:T(8,128)(2,1)}, u32[]{:S(2)}, u32[]{:S(2)}) %all-to-all-start.4) | async-done | bytes 737312 | tf_op jit(solution)/shard_map/all_to_all | solution.py:462
  231.0 1.4 fusion.42
  (98 shorter events, 15.1 us)
Async XLA Ops:
  7.2 3.3 %copy-start.11 = (bf16[128,64]{0,1:T(8,128)(2,1)S(1)}, bf16[128,64]{0,1:T(8,128)(2,1)}, u32[]{:S(2)}) copy-start(bf16[128,64]{0,1:T(8,128)(2,1)} %param.14) | copy-start | bytes 49156
  7.2 3.3 %copy-start.15 = (bf16[128,64]{0,1:T(8,128)(2,1)S(1)}, bf16[128,64]{0,1:T(8,128)(2,1)}, u32[]{:S(2)}) copy-start(bf16[128,64]{0,1:T(8,128)(2,1)} %param.15) | copy-start | bytes 49156
  7.2 7.6 %copy-start.13 = (bf16[512,45]{0,1:T(8,128)(2,1)S(1)}, bf16[512,45]{0,1:T(8,128)(2,1)}, u32[]{:S(2)}) copy-start(bf16[512,45]{0,1:T(8,128)(2,1)} %param.17) | copy-start | bytes 138244
  7.2 11.8 %copy-start.14 = (s32[128,4]{0,1:T(4,128)S(1)}, s32[128,4]{0,1:T(4,128)}, u32[]{:S(2)}) copy-start(s32[128,4]{0,1:T(4,128)} %param.21) | copy-start | bytes 6148
  7.2 12.1 %copy-start.9 = (bf16[128,360]{0,1:T(8,128)(2,1)S(1)}, bf16[128,360]{0,1:T(8,128)(2,1)}, u32[]{:S(2)}) copy-start(bf16[128,360]{0,1:T(8,128)(2,1)} %param.18) | copy-start | bytes 276484
  7.2 15.5 %copy-start.8 = (bf16[128,512]{1,0:T(8,128)(2,1)S(1)}, bf16[128,512]{1,0:T(8,128)(2,1)}, u32[]{:S(2)}) copy-start(bf16[128,512]{1,0:T(8,128)(2,1)} %param.13) | copy-start | bytes 393220
  7.2 16.3 %copy-start.16 = (f32[8]{0:T(128)S(1)}, f32[8]{0:T(128)}, u32[]{:S(2)}) copy-start(f32[8]{0:T(128)} %param.16) | copy-start | bytes 100
  10.5 12.7 %collective-permute-start = (bf16[128,128]{0,1:T(8,128)(2,1)S(1)}, bf16[128,128]{0,1:T(8,128)(2,1)S(1)}, u32[]{:S(2)}, u32[]{:S(2)}) collective-permute-start(bf16[128,128]{0,1:T(8,128)(2,1)S(1)} %pad_maximum_fusion), channel_id=1, source_target_pairs={{0,8},{8,16},{16,24},{24,32},{32,40},{40,48},{48,56},{56,64},{64,7... | collective-permute-start | bytes 98312 | tf_op jit(solution)/shard_map/ppermute | solution.py:25
  14.8 8.4 %collective-permute-start.1 = (bf16[1,45,512]{2,1,0:T(8,128)(2,1)S(1)}, bf16[1,45,512]{2,1,0:T(8,128)(2,1)S(1)}, u32[]{:S(2)}, u32[]{:S(2)}) collective-permute-start(bf16[1,45,512]{2,1,0:T(8,128)(2,1)S(1)} %bitcast.66), channel_id=1, source_target_pairs={{0,8},{8,0},{16,24},{24,16},{32,40},{40,32},{48,56},{56,48},{1,9},... | collective-permute-start | bytes 138248 | tf_op jit(solution)/shard_map/ppermute | solution.py:48
  19.3 9.1 %collective-permute-start.2 = (bf16[128,384]{0,1:T(8,128)(2,1)S(1)}, bf16[128,384]{0,1:T(8,128)(2,1)S(1)}, u32[]{:S(2)}, u32[]{:S(2)}) collective-permute-start(bf16[128,384]{0,1:T(8,128)(2,1)S(1)} %fusion.18), channel_id=1, source_target_pairs={{0,0},{1,64},{2,128},{3,192},{4,256},{5,320},{6,384},{7,448},{8,8}... | collective-permute-start | bytes 294920 | tf_op jit(solution)/shard_map/ppermute | solution.py:37
  29.6 29.3 %copy-start.17 = (f32[360]{0:T(512)S(1)}, f32[360]{0:T(512)}, u32[]{:S(2)}) copy-start(f32[360]{0:T(512)} %param.19) | copy-start | bytes 4324
  29.6 29.4 %copy-start.12 = (bf16[360,64]{0,1:T(8,128)(2,1)S(1)}, bf16[360,64]{0,1:T(8,128)(2,1)}, u32[]{:S(2)}) copy-start(bf16[360,64]{0,1:T(8,128)(2,1)} %param.20) | copy-start | bytes 138244
  29.6 34.2 %all-to-all-start = ((bf16[8,128,512]{2,1,0:T(8,128)(2,1)}), bf16[8,128,512]{2,1,0:T(8,128)(2,1)S(1)}, u32[]{:S(2)}, u32[]{:S(2)}) async-start(bf16[8,128,512]{2,1,0:T(8,128)(2,1)} %broadcast_in_dim.18), calls=%async_computation | async-start | bytes 2097152 | tf_op jit(solution)/shard_map/all_to_all | solution.py:42
  41.3 103.6 %all-gather.3.cloned.1.call-start = ((), (), s32[]{:S(2)}) async-start(), calls=%async_computation.5 | async-start | bytes 6782976 | tf_op jit(solution)/shard_map/all_gather | solution.py:76
  41.3 10.3 %collective-permute-start.3 = (bf16[2,45,512]{2,1,0:T(8,128)(2,1)S(1)}, bf16[2,45,512]{2,1,0:T(8,128)(2,1)S(1)}, u32[]{:S(2)}, u32[]{:S(2)}) collective-permute-start(bf16[2,45,512]{2,1,0:T(8,128)(2,1)S(1)} %maximum_select_fusion.3), channel_id=1, source_target_pairs={{0,16},{8,24},{16,0},{24,8},{32,48},{40,56},{48,32},{56,40},{1,17}... | collective-permute-start | bytes 276488 | tf_op jit(solution)/shard_map/ppermute | solution.py:48
  51.6 12.0 %collective-permute-start.4 = (bf16[4,45,512]{2,1,0:T(8,128)(2,1)S(1)}, bf16[4,45,512]{2,1,0:T(8,128)(2,1)S(1)}, u32[]{:S(2)}, u32[]{:S(2)}) collective-permute-start(bf16[4,45,512]{2,1,0:T(8,128)(2,1)S(1)} %maximum_select_fusion.2), channel_id=1, source_target_pairs={{0,32},{8,40},{16,48},{24,56},{32,0},{40,8},{48,16},{56,24},{1,33}... | collective-permute-start | bytes 552968 | tf_op jit(solution)/shard_map/ppermute | solution.py:48
  59.0 12.8 %collective-permute-start.5 = (bf16[80,384]{1,0:T(8,128)(2,1)S(1)}, bf16[80,384]{1,0:T(8,128)(2,1)S(1)}, u32[]{:S(2)}, u32[]{:S(2)}) collective-permute-start(bf16[80,384]{1,0:T(8,128)(2,1)S(1)} %fusion.24), channel_id=1, source_target_pairs={{0,0},{1,64},{2,128},{3,192},{4,256},{5,320},{6,384},{7,448},{8,8}... | collective-permute-start | bytes 184328 | tf_op jit(solution)/shard_map/ppermute | solution.py:37
  65.4 78.1 %copy-start.10 = (bf16[128,360]{0,1:T(8,128)(2,1)S(1)}, bf16[128,360]{0,1:T(8,128)(2,1)}, u32[]{:S(2)}) copy-start(bf16[128,360]{0,1:T(8,128)(2,1)} %param.25) | copy-start | bytes 276484
  65.4 23.3 %all-to-all-start.1 = ((bf16[8,128,384]{2,1,0:T(8,128)(2,1)}), bf16[8,128,384]{2,1,0:T(8,128)(2,1)S(1)}, u32[]{:S(2)}, u32[]{:S(2)}) async-start(bf16[8,128,384]{2,1,0:T(8,128)(2,1)} %bitcast.18), calls=%async_computation.1 | async-start | bytes 1572864 | tf_op jit(solution)/shard_map/all_to_all | solution.py:393
  71.4 114.6 %all-gather.5.cloned.1.call-start = ((), (), s32[]{:S(2)}) async-start(), calls=%async_computation.6 | async-start | bytes 3686400 | tf_op jit(solution)/shard_map/all_gather | solution.py:448
  125.1 16.5 %collective-permute-start.7 = (bf16[128,2944]{1,0:T(8,128)(2,1)S(1)}, bf16[128,2944]{1,0:T(8,128)(2,1)S(1)}, u32[]{:S(2)}, u32[]{:S(2)}) collective-permute-start(bf16[128,2944]{1,0:T(8,128)(2,1)S(1)} %get-tuple-element.26.refs_0_), channel_id=1, source_target_pairs={{0,2},{1,3},{2,0},{3,1},{4,6},{5,7},{6,4},{7,5},{8,10},{9,11},{10,... | collective-permute-start | bytes 2261000 | tf_op jit(solution)/shard_map/ppermute | solution.py:71
  128.5 16.4 %collective-permute-start.6 = (bf16[128,2944]{1,0:T(8,128)(2,1)S(1)}, bf16[128,2944]{1,0:T(8,128)(2,1)S(1)}, u32[]{:S(2)}, u32[]{:S(2)}) collective-permute-start(bf16[128,2944]{1,0:T(8,128)(2,1)S(1)} %get-tuple-element.26.refs_0_), channel_id=1, source_target_pairs={{0,1},{1,0},{2,3},{3,2},{4,5},{5,4},{6,7},{7,6},{8,9},{9,8},{10,11... | collective-permute-start | bytes 2261000 | tf_op jit(solution)/shard_map/ppermute | solution.py:67
  141.6 4.3 %collective-permute-start.8 = (bf16[128,2944]{1,0:T(8,128)(2,1)S(1)}, bf16[128,2944]{1,0:T(8,128)(2,1)}, u32[]{:S(2)}, u32[]{:S(2)}) collective-permute-start(bf16[128,2944]{1,0:T(8,128)(2,1)S(1)} %collective-permute-done.7.refs_2_), channel_id=1, source_target_pairs={{0,1},{1,0},{2,3},{3,2},{4,5},{5,4},{6,7},{7,6},{8,9},{9,8},{10,11... | collective-permute-start | bytes 2261000 | tf_op jit(solution)/shard_map/ppermute | solution.py:67
  145.8 2.3 copy-start.5
  152.2 12.1 %copy-start.6 = (bf16[1,1440,360]{2,1,0:T(8,128)(2,1)S(1)}, bf16[1,1440,360]{2,1,0:T(8,128)(2,1)}, u32[]{:S(2)}) copy-start(bf16[1,1440,360]{2,1,0:T(8,128)(2,1)} %param.24) | copy-start | bytes 3110404
  153.2 39.3 %all-to-all-start.3 = ((bf16[64,16,384]{2,1,0:T(8,128)(2,1)}), bf16[64,16,384]{2,1,0:T(8,128)(2,1)}, u32[]{:S(2)}, u32[]{:S(2)}) async-start(bf16[64,16,384]{2,1,0:T(8,128)(2,1)} %bitcast.24), calls=%async_computation.3 | async-start | bytes 1572864 | tf_op jit(solution)/shard_map/all_to_all | solution.py:434
  160.9 22.8 %collective-permute-start.9 = (bf16[128,384]{1,0:T(8,128)(2,1)S(1)}, bf16[128,384]{1,0:T(8,128)(2,1)S(1)}, u32[]{:S(2)}, u32[]{:S(2)}) collective-permute-start(bf16[128,384]{1,0:T(8,128)(2,1)S(1)} %convert_element_type.92), channel_id=1, source_target_pairs={{0,0},{1,64},{2,128},{3,192},{4,256},{5,320},{6,384},{7,448},{8,8}... | collective-permute-start | bytes 294920 | tf_op jit(solution)/shard_map/ppermute | solution.py:37
  186.0 1.9 copy-start
  187.9 1.3 copy-start.2
  189.2 17.7 %copy-start.1 = (bf16[3200,512]{1,0:T(8,128)(2,1)S(1)}, bf16[3200,512]{1,0:T(8,128)(2,1)}, u32[]{:S(2)}) copy-start(bf16[3200,512]{1,0:T(8,128)(2,1)} %all-gather.5.cloned.1.call-done.hidden_ref) | copy-start | bytes 9830404
  192.6 38.4 %all-to-all-start.4 = ((bf16[64,16,360]{2,1,0:T(8,128)(2,1)}), bf16[64,16,360]{2,1,0:T(8,128)(2,1)}, u32[]{:S(2)}, u32[]{:S(2)}) async-start(bf16[64,16,360]{2,1,0:T(8,128)(2,1)} %bitcast.54), calls=%async_computation.4 | async-start | bytes 1572864 | tf_op jit(solution)/shard_map/all_to_all | solution.py:462
  211.2 19.8 %copy-start.7 = (pred[128,1024]{1,0:T(8,128)(4,1)S(1)}, pred[128,1024]{1,0:T(8,128)(4,1)}, u32[]{:S(2)}) copy-start(pred[128,1024]{1,0:T(8,128)(4,1)} %fusion.3) | copy-start | bytes 393220
  (2 other events, 1.9 us)
Sparse Core Ops, SparseCore 0:
  48.7 74.9 all-gather.2
  153.3 32.6 all-gather.4
